TPU v7x, 32 devices: a whole 2x2x4 slice. The times are simulated.
32 devices in a mesh: grp: 2 (over y), blk: 4 (over z), sub: 4 (over x, core).
Axes of the slice: x: 2, y: 2, z: 4, core: 2. Of those that a mesh axis runs over, the one named last changes fastest.
Arguments:
- acts: bfloat16 [32, 48, 5120], P(('grp', 'blk', 'sub')), parts along dimension 0, may hold values from -6 to 6
- outgrads: bfloat16 [32, 48, 6912], P(('grp', 'blk', 'sub')), parts along dimension 0, may hold values from -6 to 6
- moment: float32 [6912, 5120], P('blk'), may hold values from 12 to 192
- counts: int32 [32], P(('grp', 'blk', 'sub')), parts along dimension 0, may hold values from 1 to 48, 576 in all
- seeds: int32 [2], replicated, may hold values from 0 to 999999
Outputs:
- sketch: float32 [32, 512, 128], P(('grp', 'blk', 'sub')), parts along dimension 0
There are 2 independent parts, one for each index of `grp`. A program takes and returns all parts, laid end to end along the dimension named above; an argument that names none is the same for every part. Nothing has to cross between parts.
Inputs may be any that keep to these rules, and one draw needn't show every extreme that they name: Each example has 1 to 48 live tokens; some example of each group has 48; the counts of one group's 16 examples sum to 3 * 16 * 48 // 4 (the printed array holds all groups one after another, each with this sum).
All inputs are finite; a program needn't handle non-finite values.
Results may differ from a plain program's by a relative error of at most 0.0042.
Values may be sent and summed in bfloat16 or wider, within the bound.
No kernel may reach another device: no remote copies, remote signals or barrier semaphores. Data moves between devices by JAX's collectives and lax.ppermute only.
A program may use at most 320 MiB of HBM per device.

v0:
```python
import math

import jax
import jax.numpy as jnp
from jax import lax
from jax.sharding import PartitionSpec as P

D = 5120
FW = 6912
KR = 512
KC = 128


def rademacher(row_index, col_index, seed_value):
    hashed = (
        row_index[:, None] * 1597334677 + col_index[None, :] * 668265263 + seed_value * 374761393
    )
    hashed = hashed ^ hashed >> 15
    hashed = hashed * 1274126177
    hashed = hashed ^ hashed >> 13
    return (1 - 2 * (hashed >> 7 & 1)).astype(jnp.float32)


def shards(acts, outgrads, moment, counts, seeds):
    row_count = moment.shape[0]
    inside = (
        lax.broadcasted_iota(jnp.int32, (acts.shape[0], acts.shape[1], 1), 1)
        < counts[:, None, None]
    )
    masked = jnp.where(inside, outgrads, jnp.zeros((), outgrads.dtype))
    rows_in = lax.all_to_all(masked, "blk", split_axis=2, concat_axis=0, tiled=True)
    offset = lax.axis_index("blk") * row_count
    col_proj = (
        rademacher(jnp.arange(D, dtype=jnp.int32), jnp.arange(KC, dtype=jnp.int32), seeds[1])
        / jnp.sqrt(jnp.float32(D))
    ).astype(jnp.bfloat16)
    weights = 1.0 / (jnp.sqrt(moment) + 1e-08)

    def partial_rows_of(grad_rows, act_rows):
        gradient = jnp.einsum(
            "etr,etd->erd", grad_rows, act_rows, preferred_element_type=jnp.float32
        )
        scaled = (gradient * weights[None]).astype(jnp.bfloat16)
        return jnp.einsum(
            "erd,dk->erk", scaled, col_proj, preferred_element_type=jnp.float32
        ).astype(jnp.bfloat16)

    def blocked(grad_rows, act_rows, method):
        number = grad_rows.shape[0]
        group = math.gcd(number, 4)
        if group == number:
            return method(grad_rows, act_rows)
        grad_groups = grad_rows.reshape((number // group, group) + grad_rows.shape[1:])
        act_groups = act_rows.reshape((number // group, group) + act_rows.shape[1:])
        results = lax.map(
            lambda operands: method(operands[0], operands[1]), (grad_groups, act_groups)
        )
        return results.reshape((number,) + results.shape[2:])

    row_proj = (
        rademacher(
            offset + jnp.arange(row_count, dtype=jnp.int32),
            jnp.arange(KR, dtype=jnp.int32),
            seeds[0],
        )
        / jnp.sqrt(jnp.float32(FW))
    ).astype(jnp.bfloat16)

    def project(grad_rows, act_rows):
        partial_sum = partial_rows_of(grad_rows, act_rows)
        return jnp.einsum("rj,erk->ejk", row_proj, partial_sum, preferred_element_type=jnp.float32)

    acts_all = lax.all_gather(acts, "blk", axis=0, tiled=True)
    terms = blocked(rows_in, acts_all, project)
    sketch = lax.psum_scatter(terms, "blk", scatter_dimension=0, tiled=True)
    return sketch


def solution(mesh):
    placed = (
        P(("grp", "blk", "sub"), None, None),
        P(("grp", "blk", "sub"), None, None),
        P("blk", None),
        P(("grp", "blk", "sub")),
        P(),
    )
    return jax.shard_map(
        shards,
        mesh=mesh,
        in_specs=placed,
        out_specs=P(("grp", "blk", "sub"), None, None),
        check_vma=False,
    )
```

profile of v0, /device:TPU:0, one launch (start us, length us, event | category | flops | bytes accessed | tf_op | source)
XLA Modules:
  0.0 225.1 jit_solution(7488296972390592299)
XLA Ops:
  6.5 7.6 %copy.9 = bf16[1,48,6912]{1,0,2:T(2,128)(2,1)} copy(bf16[1,48,6912]{2,1,0:T(8,128)(2,1)} %param.6) | data formatting | bytes 1327104 | tf_op args[1]
  14.8 6.3 %fusion.65 = bf16[6912,1,48]{2,1,0:T(2,128)(2,1)S(1)} fusion(bf16[1,48,6912]{1,0,2:T(2,128)(2,1)} %copy.9, pred[48]{0:T(512)(128)(4,1)S(1)} %iota_compare_fusion), kind=kLoop, calls=%fused_computation.71 | loop fusion | flops 331776 | bytes 1327152
  21.1 0.5 broadcast.55
  21.7 38.6 %reduce = bf16[6912,48]{1,0:T(8,128)(2,1)} reduce(bf16[6912,1,48]{2,1,0:T(2,128)(2,1)S(1)} %fusion.65, bf16[]{:T(256)} %broadcast.55), dimensions={1}, to_apply=%fusion.65.reduce_sub_computation | reduce | bytes 1327106
  60.3 4.7 %reshape.38 = bf16[4,2,41472]{2,1,0:T(2,128)(2,1)} reshape(bf16[6912,48]{1,0:T(8,128)(2,1)} %reduce) | data formatting | bytes 1327104
  65.0 6.3 %all-to-all-start = ((bf16[4,2,41472]{2,1,0:T(2,128)(2,1)}), bf16[4,2,41472]{2,1,0:T(2,128)(2,1)}, u32[]{:S(2)}, u32[]{:S(2)}) async-start(bf16[4,2,41472]{2,1,0:T(2,128)(2,1)} %reshape.38), calls=%async_computation | async-start | bytes 1327104 | tf_op jit(solution)/shard_map/all_to_all | solution.py:31
  71.3 0.7 all-gather.2.cloned.1.call-update
  72.0 0.0 copy-start.1
  72.0 0.2 reduce-scatter.2.cloned.1.call-start
  72.3 30.2 %add_divide_fusion = f32[1728,5120]{1,0:T(8,128)} fusion(f32[1728,5120]{1,0:T(8,128)} %param.7), kind=kLoop, calls=%fused_computation.1 | loop fusion | flops 17694720 | bytes 70778880 | tf_op jit(solution)/shard_map/div | solution.py:37
  102.4 0.6 fusion.64
  104.3 0.6 iota_multiply_fusion
  105.0 0.0 all-to-all-done
  105.0 4.1 %reshape.39 = bf16[6912,1,48]{2,1,0:T(2,128)(2,1)S(1)} reshape(bf16[4,2,41472]{2,1,0:T(2,128)(2,1)} %all-to-all-done) | data formatting | bytes 1327104
  109.0 5.4 %copy.10 = bf16[1,48,6912]{2,1,0:T(8,128)(2,1)} copy(bf16[1,48,6912]{1,0,2:T(2,128)(2,1)S(1)} %bitcast.37) | data formatting | bytes 1327104 | tf_op jit(solution)/shard_map/all_to_all | solution.py:31
  114.4 2.3 %all_to_all.14 = bf16[1,48,4,1728]{3,2,1,0:T(4,128)(2,1)S(1)} reshape(bf16[1,48,6912]{2,1,0:T(8,128)(2,1)} %copy.10) | data formatting | bytes 1327104 | tf_op jit(solution)/shard_map/all_to_all | solution.py:31
  116.8 0.0 copy-start
  116.8 4.0 %all-gather.2.cloned.1.call-done = bf16[4,48,5120]{2,1,0:T(8,128)(2,1)} async-done(((bf16[1,48,5120]{2,1,0:T(8,128)(2,1)}), bf16[4,48,5120]{2,1,0:T(8,128)(2,1)}) %all-gather.2.cloned.1.call-update) | async-done | bytes 1966096 | tf_op jit(solution)/shard_map/all_gather | solution.py:73
  120.8 38.2 %multiply_convert_fusion.clone.7 = bf16[4,1728,5120]{2,1,0:T(8,128)(2,1)} fusion(bf16[4,48,5120]{2,1,0:T(8,128)(2,1)} %all-gather.2.cloned.1.call-done, f32[1728,5120]{1,0:T(8,128)} %add_divide_fusion, bf16[1,48,4,1728]{3,2,1,0:T(4,128)(2,1)S(1)} %all_to_all.14), kind=kOutput, calls=%fused_computation.clone.clone.clone.clone.clone.2 | convolution fusion | flops 3468165120 | bytes 108797952 | tf_op jit(solution)/shard_map/etr,etd->erd/dot_general | solution.py:40
  159.0 28.0 %fusion.9 = bf16[4,1728,128]{2,1,0:T(8,128)(2,1)S(1)} fusion(s32[]{:T(128)} %bitcast.3, s32[128]{0:T(128)S(1)} %iota_multiply_fusion.2, s32[5120]{0:T(1024)S(1)} %copy-done, bf16[4,1728,5120]{2,1,0:T(8,128)(2,1)} %multiply_convert_fusion.clone.7), kind=kOutput, calls=%fused_computation.16 | convolution fusion | flops 9069756416 | bytes 72569344 | tf_op jit(solution)/shard_map/erd,dk->erk/dot_general | solution.py:44
  187.0 3.1 %fusion.31 = f32[4,512,128]{1,2,0:T(8,128)} fusion(bf16[4,1728,128]{2,1,0:T(8,128)(2,1)S(1)} %fusion.9, s32[]{:T(128)} %bitcast.5, s32[512]{0:T(512)S(1)} %iota_multiply_fusion.1, s32[1728]{0:T(1024)S(1)} %add_multiply_fusion), kind=kOutput, calls=%fused_computation.37 | convolution fusion | flops 918355968 | bytes 2827012 | tf_op jit(solution)/shard_map/rj,erk->ejk/dot_general | solution.py:71
  190.1 0.0 reduce-scatter.2.cloned.1.call-update
  190.1 26.3 %reduce-scatter.2.cloned.1.call-done = f32[1,512,128]{1,2,0:T(8,128)} async-done(((f32[4,512,128]{1,2,0:T(8,128)}), f32[1,512,128]{1,2,0:T(8,128)}) %reduce-scatter.2.cloned.1.call-update) | async-done | bytes 262160 | tf_op jit(solution)/shard_map/reduce_scatter | solution.py:75
  216.5 1.8 copy.12
  (7 shorter events, 0.0 us)
Async XLA Ops:
  65.0 40.0 %all-to-all-start = ((bf16[4,2,41472]{2,1,0:T(2,128)(2,1)}), bf16[4,2,41472]{2,1,0:T(2,128)(2,1)}, u32[]{:S(2)}, u32[]{:S(2)}) async-start(bf16[4,2,41472]{2,1,0:T(2,128)(2,1)} %reshape.38), calls=%async_computation | async-start | bytes 1327104 | tf_op jit(solution)/shard_map/all_to_all | solution.py:31
  71.3 49.5 %all-gather.2.cloned.1.call-start = ((), (), s32[]{:S(2)}) async-start(), calls=%async_computation.2 | async-start | bytes 2457600 | tf_op jit(solution)/shard_map/all_gather | solution.py:73
  72.0 30.4 %copy-start.1 = (s32[2]{0:T(128)S(1)}, s32[2]{0:T(128)}, u32[]{:S(2)}) copy-start(s32[2]{0:T(128)} %param.9) | copy-start | bytes 28
  72.0 144.4 %reduce-scatter.2.cloned.1.call-start = ((), (), s32[]{:S(2)}) async-start(), calls=%async_computation.3 | async-start | bytes 1310720 | tf_op jit(solution)/shard_map/reduce_scatter | solution.py:75
  116.8 42.2 %copy-start = (s32[5120]{0:T(1024)S(1)}, s32[5120]{0:T(1024)}, u32[]{:S(2)}) copy-start(s32[5120]{0:T(1024)} %iota_multiply_fusion) | copy-start | bytes 61444
Sparse Core Ops, SparseCore 0:
  73.7 47.0 all-gather.1
  190.3 26.1 reduce-scatter.1
where the time goes:
time: 226 us; the launch traced here: 225 us
  other arithmetic  75.8 us (34%)
  matrix products  69.3 us (31%)
  waiting for transfers between devices  31.1 us (14%)
  local copies, waits for them, and re-layouts  27 us (12%)
  between operations  15.4 us (7%)
  starting transfers between devices  6.54 us (3%)
    unnamed x2, other arithmetic  45 us
    dot_general x1, matrix products, partial_rows_of(): jnp.einsum('etr,etd->erd', grad_rows, act_rows, preferred_element_type=jn...  38.2 us
    div x1, other arithmetic, shards(): weights = 1.0 / (jnp.sqrt(moment) + 1e-08)  30.2 us
    dot_general x1, matrix products, partial_rows_of(): jnp.einsum('erd,dk->erk', scaled, col_proj, preferred_element_type=jnp.fl...  28 us
    reduce_scatter x1, waiting for transfers between devices, shards(): sketch = lax.psum_scatter(terms, 'blk', scatter_dimension=0, tiled=True)  26.3 us
    unnamed x8, local copies, waits for them, and re-layouts  16.9 us
    all_to_all x2, local copies, waits for them, and re-layouts, shards(): lax.all_to_all(masked, 'blk', split_axis=2, concat_axis=0, tiled=True)  7.72 us
    all_to_all x1, starting transfers between devices, shards(): lax.all_to_all(masked, 'blk', split_axis=2, concat_axis=0, tiled=True)  6.32 us
  transfers between devices with their start and end apart: 3, of which 2 were waited for; matrix products, arithmetic and copies ran while one was open for 18% of the time, Pallas kernels for 0%

commit v1 on v0

--- a/solution.py
+++ b/solution.py
@@ -1,14 +1,24 @@
+import functools
 import math
 
 import jax
 import jax.numpy as jnp
+import numpy as np
 from jax import lax
+from jax.experimental import pallas as pl
+from jax.experimental.pallas import tpu as pltpu
 from jax.sharding import PartitionSpec as P
 
 D = 5120
 FW = 6912
 KR = 512
 KC = 128
+F32 = jnp.float32
+BF16 = jnp.bfloat16
+VMEM = pl.BlockSpec(memory_space=pltpu.VMEM)
+SMEM = pl.BlockSpec(memory_space=pltpu.SMEM)
+HBM = pl.BlockSpec(memory_space=pltpu.HBM)
+LIMIT = 24 << 20
 
 
 def rademacher(row_index, col_index, seed_value):
@@ -21,7 +31,7 @@
     return (1 - 2 * (hashed >> 7 & 1)).astype(jnp.float32)
 
 
-def shards(acts, outgrads, moment, counts, seeds):
+def generic_shards(acts, outgrads, moment, counts, seeds):
     row_count = moment.shape[0]
     inside = (
         lax.broadcasted_iota(jnp.int32, (acts.shape[0], acts.shape[1], 1), 1)
@@ -76,6 +86,207 @@
     return sketch
 
 
+def hashed_sign(rows_part, cols_part, scale):
+    h = rows_part + cols_part
+    h = h ^ (h >> 15)
+    h = h * 1274126177
+    h = h ^ (h >> 13)
+    return jnp.where(((h >> 7) & 1) == 0, scale, -scale).astype(BF16)
+
+
+def iota_times(shape, axis, factor, first=0):
+    return (lax.broadcasted_iota(jnp.int32, shape, axis) + first) * factor
+
+
+def split_kernel(counts, place, grads, *outs):
+    tokens = grads.shape[0]
+    rows = outs[0].shape[1]
+    live = lax.broadcasted_iota(jnp.int32, (tokens, rows), 0) < counts[0]
+    for block in range(len(outs)):
+        part = grads[:, block * rows : (block + 1) * rows]
+        part = jnp.where(live, part.astype(F32), 0.0).astype(BF16)
+        for k, out in enumerate(outs):
+
+            @pl.when(place[0] == block ^ k)
+            def _():
+                out[...] = part
+
+
+def project_rows(row_proj, partial, out):
+    out[...] = jnp.dot(row_proj[...], partial[...], preferred_element_type=F32).astype(out.dtype)
+
+
+def first_kernel(
+    tile, chunk, seeds, place, grads, acts, moment, out, weights, col_proj, row_proj, grads_t, partial, sems
+):
+    rows, depth = weights.shape
+    tiles = rows // tile
+
+    def moment_copy(t):
+        part = pl.ds(pl.multiple_of(t * tile, 16), tile)
+        return pltpu.make_async_copy(moment.at[part], weights.at[part], sems.at[t])
+
+    for t in range(tiles):
+        moment_copy(t).start()
+    row_scale, col_scale = (float(np.float32(1) / np.sqrt(np.float32(n))) for n in (FW, D))
+    cols_part = iota_times((1, KC), 1, 668265263) + seeds[1] * 374761393
+
+    @pl.loop(0, depth // 256)
+    def _(c):
+        part = pl.ds(pl.multiple_of(c * 256, 256), 256)
+        rows_part = iota_times((256, 1), 0, 1597334677, c * 256)
+        col_proj[part] = hashed_sign(rows_part, cols_part, col_scale)
+
+    across = iota_times((1, rows), 1, 1597334677, place[0] * rows) + seeds[0] * 374761393
+
+    @pl.loop(0, KR // 32)
+    def _(j):
+        part = pl.ds(pl.multiple_of(j * 32, 32), 32)
+        down = iota_times((32, 1), 0, 668265263, j * 32)
+        row_proj[part] = hashed_sign(down, across, row_scale)
+
+    grads_t[...] = grads[...].astype(F32).T.astype(BF16)
+
+    @pl.loop(0, tiles)
+    def _(t):
+        moment_copy(t).wait()
+        part = pl.ds(pl.multiple_of(t * tile, 16), tile)
+        left = grads_t[part]
+        total = jnp.zeros((tile, KC), F32)
+        for c in range(0, depth, chunk):
+            cols = pl.ds(c, chunk)
+            weight = weights[part, cols]
+            weight = 1.0 / (weight * lax.rsqrt(weight) + 1e-08)
+            weights[part, cols] = weight
+            gradient = jnp.dot(left, acts[:, cols], preferred_element_type=F32)
+            scaled = (gradient * weight).astype(BF16)
+            total += jnp.dot(scaled, col_proj[cols], preferred_element_type=F32)
+        partial[part] = total.astype(BF16)
+
+    project_rows(row_proj, partial, out)
+
+
+def next_kernel(tile, chunk, place, grads_m, grads_e, acts_m, acts_e, weights, col_proj, row_proj, out, acts, grads_t, partial):
+    rows, depth = weights.shape
+    tiles = rows // tile
+    if grads_e is None:
+        grads_t[...] = grads_m[...].astype(F32).T.astype(BF16)
+        acts = acts_m
+    else:
+        middle = jnp.logical_or(place[0] == 1, place[0] == 2)
+
+        @pl.when(middle)
+        def _():
+            acts[...] = acts_m[...]
+
+        @pl.when(jnp.logical_not(middle))
+        def _():
+            acts[...] = acts_e[...]
+
+        grads_t[...] = grads_m[...].astype(F32).T.astype(BF16)
+
+    @pl.loop(0, tiles)
+    def _(t):
+        part = pl.ds(pl.multiple_of(t * tile, 16), tile)
+        left = grads_t[part]
+        total = jnp.zeros((tile, KC), F32)
+        for c in range(0, depth, chunk):
+            cols = pl.ds(c, chunk)
+            gradient = jnp.dot(left, acts[:, cols], preferred_element_type=F32)
+            scaled = (gradient * weights[part, cols]).astype(BF16)
+            total += jnp.dot(scaled, col_proj[cols], preferred_element_type=F32)
+        partial[part] = total.astype(BF16)
+
+    project_rows(row_proj, partial, out)
+
+
+def line_shards(acts, outgrads, moment, counts, seeds):
+    rows, depth = moment.shape
+    tokens = acts.shape[1]
+    tile = rows // 4
+    chunk = 256
+    acts, outgrads = acts[0], outgrads[0]
+    place = lax.axis_index("blk").astype(jnp.int32)[None]
+    cost = pl.CostEstimate(flops=4 * rows * depth * 256, bytes_accessed=rows * depth * 4, transcendentals=0)
+    params = pltpu.CompilerParams(vmem_limit_bytes=LIMIT)
+
+    swap = [(0, 1), (1, 0), (2, 3), (3, 2)]
+    two = [(0, 2), (2, 0), (1, 3), (3, 1)]
+    three = [(0, 3), (3, 0), (1, 2), (2, 1)]
+    inner = [(1, 2), (2, 1)]
+    outward = [(2, 3), (1, 0)]
+
+    def send(x, pairs):
+        return lax.ppermute(x, "blk", pairs)
+
+    near = send(acts, swap)
+    across = send(acts, inner)
+    own_g, near_g, two_g, three_g = pl.pallas_call(
+        split_kernel,
+        in_specs=[SMEM, SMEM, VMEM],
+        out_specs=[VMEM] * 4,
+        out_shape=[jax.ShapeDtypeStruct((tokens, rows), BF16)] * 4,
+    )(counts, place, outgrads)
+    near_g = send(near_g, swap)
+    two_g = send(two_g, two)
+    three_g = send(three_g, three)
+
+    own, weights, col_proj, row_proj = pl.pallas_call(
+        functools.partial(first_kernel, tile, chunk),
+        in_specs=[SMEM, SMEM, VMEM, VMEM, HBM],
+        out_specs=[VMEM] * 4,
+        out_shape=[
+            jax.ShapeDtypeStruct((KR, KC), F32),
+            pltpu.VMEM((rows, depth), F32),
+            pltpu.VMEM((depth, KC), BF16),
+            pltpu.VMEM((KR, rows), BF16),
+        ],
+        scratch_shapes=[
+            pltpu.VMEM((rows, tokens), BF16),
+            pltpu.VMEM((rows, KC), BF16),
+            pltpu.SemaphoreType.DMA((rows // tile,)),
+        ],
+        compiler_params=params,
+        cost_estimate=cost,
+    )(seeds, place, pltpu.with_memory_space_constraint(own_g, pltpu.VMEM), acts, moment)
+
+    def held(x):
+        return pltpu.with_memory_space_constraint(x, pltpu.VMEM)
+
+    def term(grads, acts_m, acts_e=None):
+        scratch = [pltpu.VMEM((rows, tokens), BF16), pltpu.VMEM((rows, KC), BF16)]
+        common = dict(
+            out_specs=VMEM,
+            out_shape=jax.ShapeDtypeStruct((KR, KC), BF16),
+            compiler_params=params,
+            cost_estimate=cost,
+        )
+        if acts_e is None:
+
+            def body(place, g, a, w, c, r, out, grads_t, partial):
+                next_kernel(tile, chunk, place, g, None, a, None, w, c, r, out, None, grads_t, partial)
+
+            return pl.pallas_call(body, in_specs=[SMEM] + [VMEM] * 5, scratch_shapes=scratch, **common)(
+                place, held(grads), held(acts_m), held(weights), held(col_proj), held(row_proj)
+            )
+
+        def body(place, g, a, b, w, c, r, out, chosen, grads_t, partial):
+            next_kernel(tile, chunk, place, g, g, a, b, w, c, r, out, chosen, grads_t, partial)
+
+        return pl.pallas_call(
+            body, in_specs=[SMEM] + [VMEM] * 6, scratch_shapes=[pltpu.VMEM((tokens, depth), BF16)] + scratch, **common
+        )(place, held(grads), held(acts_m), held(acts_e), held(weights), held(col_proj), held(row_proj))
+
+    near2 = send(near, inner)
+    across2 = send(across, outward)
+    near_term = send(term(near_g, near), swap)
+    last = send(near2, outward)
+    two_term = send(term(two_g, near2, across2), two)
+    three_term = send(term(three_g, across, last), three)
+    sketch = own + near_term.astype(F32) + two_term.astype(F32) + three_term.astype(F32)
+    return sketch[None]
+
+
 def solution(mesh):
     placed = (
         P(("grp", "blk", "sub"), None, None),
@@ -84,6 +295,11 @@
         P(("grp", "blk", "sub")),
         P(),
     )
+
+    def shards(acts, outgrads, moment, counts, seeds):
+        line = mesh.shape["blk"] == 4 and acts.shape[0] == 1 and moment.shape[0] % 64 == 0
+        return (line_shards if line else generic_shards)(acts, outgrads, moment, counts, seeds)
+
     return jax.shard_map(
         shards,
         mesh=mesh,

time: 226 us -> 109 us (0.48)
  other arithmetic: 75.8 us -> 0.76 us
  matrix products: 69.3 us -> 0 us
  Pallas kernels: 0 us -> 55.6 us
  waiting for transfers between devices: 31.1 us -> 5.8 us
  starting transfers between devices: 6.54 us -> 21.4 us
  between operations: 15.4 us -> 0.75 us
  local copies, waits for them, and re-layouts: 27 us -> 24.4 us
    dot_general x3 -> x0, matrix products: 69.3 us -> none  [the longest x1 38.2 us: partial_rows_of(): jnp.einsum('etr,etd->erd', grad_rows, act_rows, preferred_element_type=jn...]
    pallas_call x0 -> x5, Pallas kernels: none -> 55.6 us  [the longest x2 24 us: term(): pl.pallas_call(body, in_specs=[SMEM] + [VMEM] * 6, scratch_shapes=[pltpu....]
    unnamed x2 -> x0, other arithmetic: 45 us -> none
    div x1 -> x0, other arithmetic: 30.2 us -> none  [shards(): weights = 1.0 / (jnp.sqrt(moment) + 1e-08)]
    reduce_scatter x1 -> x0, waiting for transfers between devices: 26.3 us -> none  [shards(): sketch = lax.psum_scatter(terms, 'blk', scatter_dimension=0, tiled=True)]
    ppermute x0 -> x11, starting transfers between devices: none -> 21.4 us  [send(): return lax.ppermute(x, 'blk', pairs)]
    all_to_all x2 -> x0, local copies, waits for them, and re-layouts: 7.72 us -> none  [shards(): lax.all_to_all(masked, 'blk', split_axis=2, concat_axis=0, tiled=True)]
    unnamed x8 -> x12, local copies, waits for them, and re-layouts: 16.9 us -> 24.4 us
  transfers between devices with their start and end apart: 3 -> 11, of which waited for: 2 -> 1; matrix products, arithmetic and copies ran while one was open for 18% -> 0% of each run, Pallas kernels for 0% -> 51%
where the time goes in v1:
time: 109 us
  Pallas kernels  55.6 us (51%)
  local copies, waits for them, and re-layouts  24.4 us (22%)
  starting transfers between devices  21.4 us (20%)
  waiting for transfers between devices  5.8 us (5%)
    unnamed x12, local copies, waits for them, and re-layouts  24.4 us
    pallas_call x2, Pallas kernels, term(): pl.pallas_call(body, in_specs=[SMEM] + [VMEM] * 6, scratch_shapes=[pltpu....  24 us
    ppermute x11, starting transfers between devices, send(): return lax.ppermute(x, 'blk', pairs)  21.4 us
    pallas_call x1, Pallas kernels, line_shards(): pl.pallas_call(functools.partial(first_kernel, tile, chunk), in_specs=[SM...  16.3 us
    pallas_call x1, Pallas kernels, term(): pl.pallas_call(body, in_specs=[SMEM] + [VMEM] * 5, scratch_shapes=scratch...  13 us
    ppermute x11, waiting for transfers between devices, send(): return lax.ppermute(x, 'blk', pairs)  5.8 us
    pallas_call x1, Pallas kernels, line_shards(): pl.pallas_call(split_kernel, in_specs=[SMEM, SMEM, VMEM], out_specs=[VMEM...  2.35 us
  transfers between devices with their start and end apart: 11, of which 1 were waited for; matrix products, arithmetic and copies ran while one was open for 0% of the time, Pallas kernels for 51%

profile of v1, /device:TPU:0, one launch (start us, length us, event | category | flops | bytes accessed | tf_op | source)
XLA Modules:
  0.0 108.7 jit_solution(16238213980105163635)
XLA Ops:
  0.0 3.0 %collective-permute-start.1 = (bf16[48,5120]{1,0:T(8,128)(2,1)}, bf16[48,5120]{1,0:T(8,128)(2,1)}, u32[]{:S(2)}, u32[]{:S(2)}) collective-permute-start(bf16[48,5120]{1,0:T(8,128)(2,1)} %bitcast.6), channel_id=1, source_target_pairs={{0,4},{4,0},{8,12},{12,8},{1,5},{5,1},{9,13},{13,9},{2,6},{6,2},{1... | collective-permute-start | bytes 1474568 | tf_op jit(solution)/shard_map/ppermute | solution.py:220
  3.0 0.7 collective-permute-start.5
  4.4 2.3 %shard_map.55 = (bf16[48,1728]{1,0:T(8,128)(2,1)}, bf16[48,1728]{1,0:T(8,128)(2,1)}, bf16[48,1728]{1,0:T(8,128)(2,1)}, bf16[48,1728]{1,0:T(8,128)(2,1)}) custom-call(s32[1]{0:T(128)S(6)} %copy.6.counts, s32[1]{0:T(128)} %bitcast.place, bf16[48,6912]{1,0:T(8,128)(2,1)} %bitcast.5), custom_call_target="tpu_custom_call" | custom-call | tf_op jit(solution)/shard_map/pallas_call | solution.py:224
  6.7 4.4 %collective-permute-start = (bf16[48,1728]{1,0:T(8,128)(2,1)}, bf16[48,1728]{1,0:T(8,128)(2,1)S(1)}, u32[]{:S(2)}, u32[]{:S(2)}) collective-permute-start(bf16[48,1728]{1,0:T(8,128)(2,1)} %get-tuple-element.15), channel_id=1, source_target_pairs={{0,4},{4,0},{8,12},{12,8},{1,5},{5,1},{9,13},{13,9},{2,6},{6,2},{1... | collective-permute-start | bytes 497672 | tf_op jit(solution)/shard_map/ppermute | solution.py:220
  11.1 0.0 collective-permute-start.3
  11.1 2.4 %collective-permute-start.8 = (bf16[48,1728]{1,0:T(8,128)(2,1)}, bf16[48,1728]{1,0:T(8,128)(2,1)S(1)}, u32[]{:S(2)}, u32[]{:S(2)}) collective-permute-start(bf16[48,1728]{1,0:T(8,128)(2,1)} %get-tuple-element.20), channel_id=1, source_target_pairs={{0,12},{12,0},{4,8},{8,4},{1,13},{13,1},{5,9},{9,5},{2,14},{14,2},... | collective-permute-start | bytes 497672 | tf_op jit(solution)/shard_map/ppermute | solution.py:220
  13.4 0.9 copy-done.4
  14.4 16.3 %shard_map.56 = (f32[512,128]{1,0:T(8,128)}, f32[1728,5120]{1,0:T(8,128)S(1)}, bf16[5120,128]{1,0:T(8,128)(2,1)S(1)}, bf16[512,1728]{1,0:T(8,128)(2,1)S(1)}) custom-call(s32[2]{0:T(128)} %seeds.1, s32[1]{0:T(128)} %bitcast.place, bf16[48,1728]{1,0:T(8,128)(2,1)S(1)} %copy-done.4, bf16[48,5120]{1,0:T(8,128)(2,1)} %bitcast.8, f32[1728,5120]{1,0:T(8,128)} %moment.1), custom_call_target="tpu_custom_call" | custom-call | flops 9059696640 | bytes 35389440 | tf_op jit(solution)/shard_map/pallas_call | solution.py:234
  30.7 11.7 %copy-done = f32[1728,5120]{1,0:T(8,128)} copy-done((f32[1728,5120]{1,0:T(8,128)}, f32[1728,5120]{1,0:T(8,128)S(1)}, u32[]{:S(2)}) %copy-start) | copy-done | bytes 35389464
  42.3 0.7 collective-permute-start.4
  43.0 1.3 %collective-permute-start.6 = (bf16[48,5120]{1,0:T(8,128)(2,1)S(1)}, bf16[48,5120]{1,0:T(8,128)(2,1)S(1)}, u32[]{:S(2)}, u32[]{:S(2)}) collective-permute-start(bf16[48,5120]{1,0:T(8,128)(2,1)S(1)} %collective-permute-done.5.a), channel_id=1, source_target_pairs={{8,12},{4,0},{9,13},{5,1},{10,14},{6,2},{11,15},{7,3},{24,28},{20,... | collective-permute-start | bytes 1474568 | tf_op jit(solution)/shard_map/ppermute | solution.py:220
  44.3 0.8 copy-done.2
  45.1 11.1 %copy-done.1 = f32[1728,5120]{1,0:T(8,128)S(1)} copy-done((f32[1728,5120]{1,0:T(8,128)S(1)}, f32[1728,5120]{1,0:T(8,128)}, u32[]{:S(2)}) %copy-start.1) | copy-done | bytes 35389464
  56.2 13.0 %shard_map.57 = bf16[512,128]{1,0:T(8,128)(2,1)} custom-call(s32[1]{0:T(128)} %bitcast.place, bf16[48,1728]{1,0:T(8,128)(2,1)S(1)} %collective-permute-done.g, bf16[48,5120]{1,0:T(8,128)(2,1)} %collective-permute-done.1.a, f32[1728,5120]{1,0:T(8,128)S(1)} %copy-done.1, bf16[5120,128]{1,0:T(8,128)(2,1)S(1)} %get-tuple-element.17.c, ...), custom_call_target="tpu_custom_call" | custom-call | flops 9059696640 | bytes 35389440 | tf_op jit(solution)/shard_map/pallas_call | solution.py:269
  69.2 2.7 %collective-permute-start.2 = (bf16[512,128]{1,0:T(8,128)(2,1)}, bf16[512,128]{1,0:T(8,128)(2,1)S(1)}, u32[]{:S(2)}, u32[]{:S(2)}) collective-permute-start(bf16[512,128]{1,0:T(8,128)(2,1)} %shard_map.57), channel_id=1, source_target_pairs={{0,4},{4,0},{8,12},{12,8},{1,5},{5,1},{9,13},{13,9},{2,6},{6,2},{1... | collective-permute-start | bytes 393224 | tf_op jit(solution)/shard_map/ppermute | solution.py:220
  71.8 0.0 collective-permute-done.4.a
  71.8 1.3 %collective-permute-start.9 = (bf16[48,5120]{1,0:T(8,128)(2,1)S(1)}, bf16[48,5120]{1,0:T(8,128)(2,1)S(1)}, u32[]{:S(2)}, u32[]{:S(2)}) collective-permute-start(bf16[48,5120]{1,0:T(8,128)(2,1)S(1)} %collective-permute-done.4.a), channel_id=1, source_target_pairs={{8,12},{4,0},{9,13},{5,1},{10,14},{6,2},{11,15},{7,3},{24,28},{20,... | collective-permute-start | bytes 1474568 | tf_op jit(solution)/shard_map/ppermute | solution.py:220
  73.1 0.0 collective-permute-done.3.g
  73.1 11.9 %shard_map.58 = bf16[512,128]{1,0:T(8,128)(2,1)} custom-call(s32[1]{0:T(128)} %bitcast.place, bf16[48,1728]{1,0:T(8,128)(2,1)S(1)} %collective-permute-done.3.g, bf16[48,5120]{1,0:T(8,128)(2,1)S(1)} %collective-permute-done.4.a, bf16[48,5120]{1,0:T(8,128)(2,1)S(1)} %collective-permute-done.6.b, f32[1728,5120]{1,0:T(8,128)S(1)} %copy-done.1, ...), custom_call_target="tpu_custom_call" | custom-call | flops 9059696640 | bytes 35389440 | tf_op jit(solution)/shard_map/pallas_call | solution.py:276
  85.1 3.8 %collective-permute-start.7 = (bf16[512,128]{1,0:T(8,128)(2,1)}, bf16[512,128]{1,0:T(8,128)(2,1)S(1)}, u32[]{:S(2)}, u32[]{:S(2)}) collective-permute-start(bf16[512,128]{1,0:T(8,128)(2,1)} %shard_map.58), channel_id=1, source_target_pairs={{0,8},{8,0},{4,12},{12,4},{1,9},{9,1},{5,13},{13,5},{2,10},{10,2},... | collective-permute-start | bytes 393224 | tf_op jit(solution)/shard_map/ppermute | solution.py:220
  88.9 12.1 %shard_map.59 = bf16[512,128]{1,0:T(8,128)(2,1)} custom-call(s32[1]{0:T(128)} %bitcast.place, bf16[48,1728]{1,0:T(8,128)(2,1)S(1)} %collective-permute-done.8.g, bf16[48,5120]{1,0:T(8,128)(2,1)S(1)} %copy-done.3, bf16[48,5120]{1,0:T(8,128)(2,1)S(1)} %collective-permute-done.9.b, f32[1728,5120]{1,0:T(8,128)S(1)} %copy-done.1, ...), custom_call_target="tpu_custom_call" | custom-call | flops 9059696640 | bytes 35389440 | tf_op jit(solution)/shard_map/pallas_call | solution.py:276
  101.0 1.2 %collective-permute-start.10 = (bf16[512,128]{1,0:T(8,128)(2,1)}, bf16[512,128]{1,0:T(8,128)(2,1)S(1)}, u32[]{:S(2)}, u32[]{:S(2)}) collective-permute-start(bf16[512,128]{1,0:T(8,128)(2,1)} %shard_map.59), channel_id=1, source_target_pairs={{0,12},{12,0},{4,8},{8,4},{1,13},{13,1},{5,9},{9,5},{2,14},{14,2},... | collective-permute-start | bytes 393224 | tf_op jit(solution)/shard_map/ppermute | solution.py:220
  102.2 5.8 %collective-permute-done.10 = bf16[512,128]{1,0:T(8,128)(2,1)S(1)} collective-permute-done((bf16[512,128]{1,0:T(8,128)(2,1)}, bf16[512,128]{1,0:T(8,128)(2,1)S(1)}, u32[]{:S(2)}, u32[]{:S(2)}) %collective-permute-start.10) | collective-permute-done | bytes 131104 | tf_op jit(solution)/shard_map/ppermute | solution.py:220
  108.0 0.8 add_bitcast_fusion
  (16 shorter events, 0.0 us)
Async XLA Ops:
  0.0 42.3 %collective-permute-start.1 = (bf16[48,5120]{1,0:T(8,128)(2,1)}, bf16[48,5120]{1,0:T(8,128)(2,1)}, u32[]{:S(2)}, u32[]{:S(2)}) collective-permute-start(bf16[48,5120]{1,0:T(8,128)(2,1)} %bitcast.6), channel_id=1, source_target_pairs={{0,4},{4,0},{8,12},{12,8},{1,5},{5,1},{9,13},{13,9},{2,6},{6,2},{1... | collective-permute-start | bytes 1474568 | tf_op jit(solution)/shard_map/ppermute | solution.py:220
  3.0 40.0 %collective-permute-start.5 = (bf16[48,5120]{1,0:T(8,128)(2,1)}, bf16[48,5120]{1,0:T(8,128)(2,1)S(1)}, u32[]{:S(2)}, u32[]{:S(2)}) collective-permute-start(bf16[48,5120]{1,0:T(8,128)(2,1)} %bitcast.7), channel_id=1, source_target_pairs={{4,8},{8,4},{5,9},{9,5},{6,10},{10,6},{7,11},{11,7},{20,24},{24,20... | collective-permute-start | bytes 1474568 | tf_op jit(solution)/shard_map/ppermute | solution.py:220
  6.7 38.4 %collective-permute-start = (bf16[48,1728]{1,0:T(8,128)(2,1)}, bf16[48,1728]{1,0:T(8,128)(2,1)S(1)}, u32[]{:S(2)}, u32[]{:S(2)}) collective-permute-start(bf16[48,1728]{1,0:T(8,128)(2,1)} %get-tuple-element.15), channel_id=1, source_target_pairs={{0,4},{4,0},{8,12},{12,8},{1,5},{5,1},{9,13},{13,9},{2,6},{6,2},{1... | collective-permute-start | bytes 497672 | tf_op jit(solution)/shard_map/ppermute | solution.py:220
  11.1 62.0 %collective-permute-start.3 = (bf16[48,1728]{1,0:T(8,128)(2,1)}, bf16[48,1728]{1,0:T(8,128)(2,1)S(1)}, u32[]{:S(2)}, u32[]{:S(2)}) collective-permute-start(bf16[48,1728]{1,0:T(8,128)(2,1)} %get-tuple-element.19), channel_id=1, source_target_pairs={{0,8},{8,0},{4,12},{12,4},{1,9},{9,1},{5,13},{13,5},{2,10},{10,2},... | collective-permute-start | bytes 497672 | tf_op jit(solution)/shard_map/ppermute | solution.py:220
  11.1 77.8 %collective-permute-start.8 = (bf16[48,1728]{1,0:T(8,128)(2,1)}, bf16[48,1728]{1,0:T(8,128)(2,1)S(1)}, u32[]{:S(2)}, u32[]{:S(2)}) collective-permute-start(bf16[48,1728]{1,0:T(8,128)(2,1)} %get-tuple-element.20), channel_id=1, source_target_pairs={{0,12},{12,0},{4,8},{8,4},{1,13},{13,1},{5,9},{9,5},{2,14},{14,2},... | collective-permute-start | bytes 497672 | tf_op jit(solution)/shard_map/ppermute | solution.py:220
  13.4 0.9 copy-start.4
  30.7 11.7 %copy-start = (f32[1728,5120]{1,0:T(8,128)}, f32[1728,5120]{1,0:T(8,128)S(1)}, u32[]{:S(2)}) copy-start(f32[1728,5120]{1,0:T(8,128)S(1)} %get-tuple-element.16.w) | copy-start | bytes 106168320
  42.3 29.5 %collective-permute-start.4 = (bf16[48,5120]{1,0:T(8,128)(2,1)}, bf16[48,5120]{1,0:T(8,128)(2,1)S(1)}, u32[]{:S(2)}, u32[]{:S(2)}) collective-permute-start(bf16[48,5120]{1,0:T(8,128)(2,1)} %collective-permute-done.1.a), channel_id=1, source_target_pairs={{4,8},{8,4},{5,9},{9,5},{6,10},{10,6},{7,11},{11,7},{20,24},{24,20... | collective-permute-start | bytes 1474568 | tf_op jit(solution)/shard_map/ppermute | solution.py:220
  43.0 30.1 %collective-permute-start.6 = (bf16[48,5120]{1,0:T(8,128)(2,1)S(1)}, bf16[48,5120]{1,0:T(8,128)(2,1)S(1)}, u32[]{:S(2)}, u32[]{:S(2)}) collective-permute-start(bf16[48,5120]{1,0:T(8,128)(2,1)S(1)} %collective-permute-done.5.a), channel_id=1, source_target_pairs={{8,12},{4,0},{9,13},{5,1},{10,14},{6,2},{11,15},{7,3},{24,28},{20,... | collective-permute-start | bytes 1474568 | tf_op jit(solution)/shard_map/ppermute | solution.py:220
  44.3 0.8 copy-start.2
  45.1 11.1 %copy-start.1 = (f32[1728,5120]{1,0:T(8,128)S(1)}, f32[1728,5120]{1,0:T(8,128)}, u32[]{:S(2)}) copy-start(f32[1728,5120]{1,0:T(8,128)} %copy-done) | copy-start | bytes 106168320
  56.2 32.7 %copy-start.3 = (bf16[48,5120]{1,0:T(8,128)(2,1)S(1)}, bf16[48,5120]{1,0:T(8,128)(2,1)}, u32[]{:S(2)}) copy-start(bf16[48,5120]{1,0:T(8,128)(2,1)} %copy-done.2) | copy-start | bytes 1474564
  69.2 38.8 %copy-start.5 = (f32[512,128]{1,0:T(8,128)S(1)}, f32[512,128]{1,0:T(8,128)}, u32[]{:S(2)}) copy-start(f32[512,128]{1,0:T(8,128)} %get-tuple-element.14) | copy-start | bytes 786436
  69.2 33.0 %collective-permute-start.2 = (bf16[512,128]{1,0:T(8,128)(2,1)}, bf16[512,128]{1,0:T(8,128)(2,1)S(1)}, u32[]{:S(2)}, u32[]{:S(2)}) collective-permute-start(bf16[512,128]{1,0:T(8,128)(2,1)} %shard_map.57), channel_id=1, source_target_pairs={{0,4},{4,0},{8,12},{12,8},{1,5},{5,1},{9,13},{13,9},{2,6},{6,2},{1... | collective-permute-start | bytes 393224 | tf_op jit(solution)/shard_map/ppermute | solution.py:220
  71.8 17.1 %collective-permute-start.9 = (bf16[48,5120]{1,0:T(8,128)(2,1)S(1)}, bf16[48,5120]{1,0:T(8,128)(2,1)S(1)}, u32[]{:S(2)}, u32[]{:S(2)}) collective-permute-start(bf16[48,5120]{1,0:T(8,128)(2,1)S(1)} %collective-permute-done.4.a), channel_id=1, source_target_pairs={{8,12},{4,0},{9,13},{5,1},{10,14},{6,2},{11,15},{7,3},{24,28},{20,... | collective-permute-start | bytes 1474568 | tf_op jit(solution)/shard_map/ppermute | solution.py:220
  85.1 17.1 %collective-permute-start.7 = (bf16[512,128]{1,0:T(8,128)(2,1)}, bf16[512,128]{1,0:T(8,128)(2,1)S(1)}, u32[]{:S(2)}, u32[]{:S(2)}) collective-permute-start(bf16[512,128]{1,0:T(8,128)(2,1)} %shard_map.58), channel_id=1, source_target_pairs={{0,8},{8,0},{4,12},{12,4},{1,9},{9,1},{5,13},{13,5},{2,10},{10,2},... | collective-permute-start | bytes 393224 | tf_op jit(solution)/shard_map/ppermute | solution.py:220
  101.0 7.0 %collective-permute-start.10 = (bf16[512,128]{1,0:T(8,128)(2,1)}, bf16[512,128]{1,0:T(8,128)(2,1)S(1)}, u32[]{:S(2)}, u32[]{:S(2)}) collective-permute-start(bf16[512,128]{1,0:T(8,128)(2,1)} %shard_map.59), channel_id=1, source_target_pairs={{0,12},{12,0},{4,8},{8,4},{1,13},{13,1},{5,9},{9,5},{2,14},{14,2},... | collective-permute-start | bytes 393224 | tf_op jit(solution)/shard_map/ppermute | solution.py:220

commit v2 on v1

--- a/solution.py
+++ b/solution.py
@@ -248,7 +248,7 @@
         ],
         compiler_params=params,
         cost_estimate=cost,
-    )(seeds, place, pltpu.with_memory_space_constraint(own_g, pltpu.VMEM), acts, moment)
+    )(seeds, place, own_g, acts, moment)
 
     def held(x):
         return pltpu.with_memory_space_constraint(x, pltpu.VMEM)

time: 109 us -> 85.4 us (0.78)
  local copies, waits for them, and re-layouts: 24.4 us -> 0.77 us
    unnamed x12 -> x6, local copies, waits for them, and re-layouts: 24.4 us -> 0.77 us
  transfers between devices with their start and end apart: 11 -> 11, of which waited for: 1 -> 1; matrix products, arithmetic and copies ran while one was open for 0% -> 0% of each run, Pallas kernels for 51% -> 65%
where the time goes in v2:
time: 85.4 us; the launch traced here: 85.2 us
  Pallas kernels  55.7 us (65%)
  starting transfers between devices  21.4 us (25%)
  waiting for transfers between devices  5.81 us (7%)
    pallas_call x2, Pallas kernels, term(): pl.pallas_call(body, in_specs=[SMEM] + [VMEM] * 6, scratch_shapes=[pltpu....  24 us
    ppermute x11, starting transfers between devices, send(): return lax.ppermute(x, 'blk', pairs)  21.4 us
    pallas_call x1, Pallas kernels, line_shards(): pl.pallas_call(functools.partial(first_kernel, tile, chunk), in_specs=[SM...  16.4 us
    pallas_call x1, Pallas kernels, term(): pl.pallas_call(body, in_specs=[SMEM] + [VMEM] * 5, scratch_shapes=scratch...  12.9 us
    ppermute x11, waiting for transfers between devices, send(): return lax.ppermute(x, 'blk', pairs)  5.81 us
    pallas_call x1, Pallas kernels, line_shards(): pl.pallas_call(split_kernel, in_specs=[SMEM, SMEM, VMEM], out_specs=[VMEM...  2.38 us
  transfers between devices with their start and end apart: 11, of which 1 were waited for; matrix products, arithmetic and copies ran while one was open for 0% of the time, Pallas kernels for 65%

profile of v2, /device:TPU:0, one launch (start us, length us, event | category | flops | bytes accessed | tf_op | source)
XLA Modules:
  0.0 85.2 jit_solution(13199470143234998394)
XLA Ops:
  0.0 3.0 %collective-permute-start.1 = (bf16[48,5120]{1,0:T(8,128)(2,1)}, bf16[48,5120]{1,0:T(8,128)(2,1)}, u32[]{:S(2)}, u32[]{:S(2)}) collective-permute-start(bf16[48,5120]{1,0:T(8,128)(2,1)} %bitcast.6), channel_id=1, source_target_pairs={{0,4},{4,0},{8,12},{12,8},{1,5},{5,1},{9,13},{13,9},{2,6},{6,2},{1... | collective-permute-start | bytes 1474568 | tf_op jit(solution)/shard_map/ppermute | solution.py:220
  3.0 0.7 collective-permute-start.5
  4.4 2.4 %shard_map.55 = (bf16[48,1728]{1,0:T(8,128)(2,1)}, bf16[48,1728]{1,0:T(8,128)(2,1)}, bf16[48,1728]{1,0:T(8,128)(2,1)}, bf16[48,1728]{1,0:T(8,128)(2,1)}) custom-call(s32[1]{0:T(128)S(6)} %copy.6.counts, s32[1]{0:T(128)} %bitcast.place, bf16[48,6912]{1,0:T(8,128)(2,1)} %bitcast.5), custom_call_target="tpu_custom_call" | custom-call | tf_op jit(solution)/shard_map/pallas_call | solution.py:224
  6.7 4.4 %collective-permute-start = (bf16[48,1728]{1,0:T(8,128)(2,1)}, bf16[48,1728]{1,0:T(8,128)(2,1)S(1)}, u32[]{:S(2)}, u32[]{:S(2)}) collective-permute-start(bf16[48,1728]{1,0:T(8,128)(2,1)} %get-tuple-element.15), channel_id=1, source_target_pairs={{0,4},{4,0},{8,12},{12,8},{1,5},{5,1},{9,13},{13,9},{2,6},{6,2},{1... | collective-permute-start | bytes 497672 | tf_op jit(solution)/shard_map/ppermute | solution.py:220
  11.1 0.0 collective-permute-start.3
  11.1 2.4 %collective-permute-start.8 = (bf16[48,1728]{1,0:T(8,128)(2,1)}, bf16[48,1728]{1,0:T(8,128)(2,1)S(1)}, u32[]{:S(2)}, u32[]{:S(2)}) collective-permute-start(bf16[48,1728]{1,0:T(8,128)(2,1)} %get-tuple-element.20), channel_id=1, source_target_pairs={{0,12},{12,0},{4,8},{8,4},{1,13},{13,1},{5,9},{9,5},{2,14},{14,2},... | collective-permute-start | bytes 497672 | tf_op jit(solution)/shard_map/ppermute | solution.py:220
  13.5 16.4 %shard_map.56 = (f32[512,128]{1,0:T(8,128)}, f32[1728,5120]{1,0:T(8,128)S(1)}, bf16[5120,128]{1,0:T(8,128)(2,1)S(1)}, bf16[512,1728]{1,0:T(8,128)(2,1)S(1)}) custom-call(s32[2]{0:T(128)} %seeds.1, s32[1]{0:T(128)} %bitcast.place, bf16[48,1728]{1,0:T(8,128)(2,1)} %get-tuple-element.13.grads, bf16[48,5120]{1,0:T(8,128)(2,1)} %bitcast.8, f32[1728,5120]{1,0:T(8,128)} %moment.1), custom_call_target="tpu_custom_call" | custom-call | flops 9059696640 | bytes 35389440 | tf_op jit(solution)/shard_map/pallas_call | solution.py:234
  29.9 0.7 collective-permute-start.4
  30.6 0.0 collective-permute-done.5.a
  30.6 1.3 %collective-permute-start.6 = (bf16[48,5120]{1,0:T(8,128)(2,1)S(1)}, bf16[48,5120]{1,0:T(8,128)(2,1)S(1)}, u32[]{:S(2)}, u32[]{:S(2)}) collective-permute-start(bf16[48,5120]{1,0:T(8,128)(2,1)S(1)} %collective-permute-done.5.a), channel_id=1, source_target_pairs={{8,12},{4,0},{9,13},{5,1},{10,14},{6,2},{11,15},{7,3},{24,28},{20,... | collective-permute-start | bytes 1474568 | tf_op jit(solution)/shard_map/ppermute | solution.py:220
  31.9 0.8 copy-done
  32.7 0.0 collective-permute-done.g
  32.7 12.9 %shard_map.57 = bf16[512,128]{1,0:T(8,128)(2,1)} custom-call(s32[1]{0:T(128)} %bitcast.place, bf16[48,1728]{1,0:T(8,128)(2,1)S(1)} %collective-permute-done.g, bf16[48,5120]{1,0:T(8,128)(2,1)} %collective-permute-done.1.a, f32[1728,5120]{1,0:T(8,128)S(1)} %get-tuple-element.16.w, bf16[5120,128]{1,0:T(8,128)(2,1)S(1)} %get-tuple-element.17.c, ...), custom_call_target="tpu_custom_call" | custom-call | flops 9059696640 | bytes 35389440 | tf_op jit(solution)/shard_map/pallas_call | solution.py:269
  45.6 2.7 %collective-permute-start.2 = (bf16[512,128]{1,0:T(8,128)(2,1)}, bf16[512,128]{1,0:T(8,128)(2,1)S(1)}, u32[]{:S(2)}, u32[]{:S(2)}) collective-permute-start(bf16[512,128]{1,0:T(8,128)(2,1)} %shard_map.57), channel_id=1, source_target_pairs={{0,4},{4,0},{8,12},{12,8},{1,5},{5,1},{9,13},{13,9},{2,6},{6,2},{1... | collective-permute-start | bytes 393224 | tf_op jit(solution)/shard_map/ppermute | solution.py:220
  48.3 1.3 %collective-permute-start.9 = (bf16[48,5120]{1,0:T(8,128)(2,1)S(1)}, bf16[48,5120]{1,0:T(8,128)(2,1)S(1)}, u32[]{:S(2)}, u32[]{:S(2)}) collective-permute-start(bf16[48,5120]{1,0:T(8,128)(2,1)S(1)} %collective-permute-done.4.a), channel_id=1, source_target_pairs={{8,12},{4,0},{9,13},{5,1},{10,14},{6,2},{11,15},{7,3},{24,28},{20,... | collective-permute-start | bytes 1474568 | tf_op jit(solution)/shard_map/ppermute | solution.py:220
  49.6 0.0 collective-permute-done.6.b
  49.6 11.9 %shard_map.58 = bf16[512,128]{1,0:T(8,128)(2,1)} custom-call(s32[1]{0:T(128)} %bitcast.place, bf16[48,1728]{1,0:T(8,128)(2,1)S(1)} %collective-permute-done.3.g, bf16[48,5120]{1,0:T(8,128)(2,1)S(1)} %collective-permute-done.4.a, bf16[48,5120]{1,0:T(8,128)(2,1)S(1)} %collective-permute-done.6.b, f32[1728,5120]{1,0:T(8,128)S(1)} %get-tuple-element.16.w, ...), custom_call_target="tpu_custom_call" | custom-call | flops 9059696640 | bytes 35389440 | tf_op jit(solution)/shard_map/pallas_call | solution.py:276
  61.5 3.8 %collective-permute-start.7 = (bf16[512,128]{1,0:T(8,128)(2,1)}, bf16[512,128]{1,0:T(8,128)(2,1)S(1)}, u32[]{:S(2)}, u32[]{:S(2)}) collective-permute-start(bf16[512,128]{1,0:T(8,128)(2,1)} %shard_map.58), channel_id=1, source_target_pairs={{0,8},{8,0},{4,12},{12,4},{1,9},{9,1},{5,13},{13,5},{2,10},{10,2},... | collective-permute-start | bytes 393224 | tf_op jit(solution)/shard_map/ppermute | solution.py:220
  65.3 0.0 collective-permute-done.8.g
  65.3 0.0 collective-permute-done.9.b
  65.3 12.1 %shard_map.59 = bf16[512,128]{1,0:T(8,128)(2,1)} custom-call(s32[1]{0:T(128)} %bitcast.place, bf16[48,1728]{1,0:T(8,128)(2,1)S(1)} %collective-permute-done.8.g, bf16[48,5120]{1,0:T(8,128)(2,1)S(1)} %copy-done.1, bf16[48,5120]{1,0:T(8,128)(2,1)S(1)} %collective-permute-done.9.b, f32[1728,5120]{1,0:T(8,128)S(1)} %get-tuple-element.16.w, ...), custom_call_target="tpu_custom_call" | custom-call | flops 9059696640 | bytes 35389440 | tf_op jit(solution)/shard_map/pallas_call | solution.py:276
  77.4 1.2 %collective-permute-start.10 = (bf16[512,128]{1,0:T(8,128)(2,1)}, bf16[512,128]{1,0:T(8,128)(2,1)S(1)}, u32[]{:S(2)}, u32[]{:S(2)}) collective-permute-start(bf16[512,128]{1,0:T(8,128)(2,1)} %shard_map.59), channel_id=1, source_target_pairs={{0,12},{12,0},{4,8},{8,4},{1,13},{13,1},{5,9},{9,5},{2,14},{14,2},... | collective-permute-start | bytes 393224 | tf_op jit(solution)/shard_map/ppermute | solution.py:220
  78.6 5.8 %collective-permute-done.10 = bf16[512,128]{1,0:T(8,128)(2,1)S(1)} collective-permute-done((bf16[512,128]{1,0:T(8,128)(2,1)}, bf16[512,128]{1,0:T(8,128)(2,1)S(1)}, u32[]{:S(2)}, u32[]{:S(2)}) %collective-permute-start.10) | collective-permute-done | bytes 131104 | tf_op jit(solution)/shard_map/ppermute | solution.py:220
  84.4 0.8 add_bitcast_fusion
  (10 shorter events, 0.0 us)
Async XLA Ops:
  0.0 29.9 %collective-permute-start.1 = (bf16[48,5120]{1,0:T(8,128)(2,1)}, bf16[48,5120]{1,0:T(8,128)(2,1)}, u32[]{:S(2)}, u32[]{:S(2)}) collective-permute-start(bf16[48,5120]{1,0:T(8,128)(2,1)} %bitcast.6), channel_id=1, source_target_pairs={{0,4},{4,0},{8,12},{12,8},{1,5},{5,1},{9,13},{13,9},{2,6},{6,2},{1... | collective-permute-start | bytes 1474568 | tf_op jit(solution)/shard_map/ppermute | solution.py:220
  3.0 27.6 %collective-permute-start.5 = (bf16[48,5120]{1,0:T(8,128)(2,1)}, bf16[48,5120]{1,0:T(8,128)(2,1)S(1)}, u32[]{:S(2)}, u32[]{:S(2)}) collective-permute-start(bf16[48,5120]{1,0:T(8,128)(2,1)} %bitcast.7), channel_id=1, source_target_pairs={{4,8},{8,4},{5,9},{9,5},{6,10},{10,6},{7,11},{11,7},{20,24},{24,20... | collective-permute-start | bytes 1474568 | tf_op jit(solution)/shard_map/ppermute | solution.py:220
  6.7 25.9 %collective-permute-start = (bf16[48,1728]{1,0:T(8,128)(2,1)}, bf16[48,1728]{1,0:T(8,128)(2,1)S(1)}, u32[]{:S(2)}, u32[]{:S(2)}) collective-permute-start(bf16[48,1728]{1,0:T(8,128)(2,1)} %get-tuple-element.15), channel_id=1, source_target_pairs={{0,4},{4,0},{8,12},{12,8},{1,5},{5,1},{9,13},{13,9},{2,6},{6,2},{1... | collective-permute-start | bytes 497672 | tf_op jit(solution)/shard_map/ppermute | solution.py:220
  11.1 38.5 %collective-permute-start.3 = (bf16[48,1728]{1,0:T(8,128)(2,1)}, bf16[48,1728]{1,0:T(8,128)(2,1)S(1)}, u32[]{:S(2)}, u32[]{:S(2)}) collective-permute-start(bf16[48,1728]{1,0:T(8,128)(2,1)} %get-tuple-element.19), channel_id=1, source_target_pairs={{0,8},{8,0},{4,12},{12,4},{1,9},{9,1},{5,13},{13,5},{2,10},{10,2},... | collective-permute-start | bytes 497672 | tf_op jit(solution)/shard_map/ppermute | solution.py:220
  11.1 54.2 %collective-permute-start.8 = (bf16[48,1728]{1,0:T(8,128)(2,1)}, bf16[48,1728]{1,0:T(8,128)(2,1)S(1)}, u32[]{:S(2)}, u32[]{:S(2)}) collective-permute-start(bf16[48,1728]{1,0:T(8,128)(2,1)} %get-tuple-element.20), channel_id=1, source_target_pairs={{0,12},{12,0},{4,8},{8,4},{1,13},{13,1},{5,9},{9,5},{2,14},{14,2},... | collective-permute-start | bytes 497672 | tf_op jit(solution)/shard_map/ppermute | solution.py:220
  29.9 18.4 %collective-permute-start.4 = (bf16[48,5120]{1,0:T(8,128)(2,1)}, bf16[48,5120]{1,0:T(8,128)(2,1)S(1)}, u32[]{:S(2)}, u32[]{:S(2)}) collective-permute-start(bf16[48,5120]{1,0:T(8,128)(2,1)} %collective-permute-done.1.a), channel_id=1, source_target_pairs={{4,8},{8,4},{5,9},{9,5},{6,10},{10,6},{7,11},{11,7},{20,24},{24,20... | collective-permute-start | bytes 1474568 | tf_op jit(solution)/shard_map/ppermute | solution.py:220
  30.6 19.0 %collective-permute-start.6 = (bf16[48,5120]{1,0:T(8,128)(2,1)S(1)}, bf16[48,5120]{1,0:T(8,128)(2,1)S(1)}, u32[]{:S(2)}, u32[]{:S(2)}) collective-permute-start(bf16[48,5120]{1,0:T(8,128)(2,1)S(1)} %collective-permute-done.5.a), channel_id=1, source_target_pairs={{8,12},{4,0},{9,13},{5,1},{10,14},{6,2},{11,15},{7,3},{24,28},{20,... | collective-permute-start | bytes 1474568 | tf_op jit(solution)/shard_map/ppermute | solution.py:220
  31.9 0.8 copy-start
  32.7 32.7 %copy-start.1 = (bf16[48,5120]{1,0:T(8,128)(2,1)S(1)}, bf16[48,5120]{1,0:T(8,128)(2,1)}, u32[]{:S(2)}) copy-start(bf16[48,5120]{1,0:T(8,128)(2,1)} %copy-done) | copy-start | bytes 1474564
  45.6 38.8 %copy-start.2 = (f32[512,128]{1,0:T(8,128)S(1)}, f32[512,128]{1,0:T(8,128)}, u32[]{:S(2)}) copy-start(f32[512,128]{1,0:T(8,128)} %get-tuple-element.14) | copy-start | bytes 786436
  45.6 33.0 %collective-permute-start.2 = (bf16[512,128]{1,0:T(8,128)(2,1)}, bf16[512,128]{1,0:T(8,128)(2,1)S(1)}, u32[]{:S(2)}, u32[]{:S(2)}) collective-permute-start(bf16[512,128]{1,0:T(8,128)(2,1)} %shard_map.57), channel_id=1, source_target_pairs={{0,4},{4,0},{8,12},{12,8},{1,5},{5,1},{9,13},{13,9},{2,6},{6,2},{1... | collective-permute-start | bytes 393224 | tf_op jit(solution)/shard_map/ppermute | solution.py:220
  48.3 17.1 %collective-permute-start.9 = (bf16[48,5120]{1,0:T(8,128)(2,1)S(1)}, bf16[48,5120]{1,0:T(8,128)(2,1)S(1)}, u32[]{:S(2)}, u32[]{:S(2)}) collective-permute-start(bf16[48,5120]{1,0:T(8,128)(2,1)S(1)} %collective-permute-done.4.a), channel_id=1, source_target_pairs={{8,12},{4,0},{9,13},{5,1},{10,14},{6,2},{11,15},{7,3},{24,28},{20,... | collective-permute-start | bytes 1474568 | tf_op jit(solution)/shard_map/ppermute | solution.py:220
  61.5 17.1 %collective-permute-start.7 = (bf16[512,128]{1,0:T(8,128)(2,1)}, bf16[512,128]{1,0:T(8,128)(2,1)S(1)}, u32[]{:S(2)}, u32[]{:S(2)}) collective-permute-start(bf16[512,128]{1,0:T(8,128)(2,1)} %shard_map.58), channel_id=1, source_target_pairs={{0,8},{8,0},{4,12},{12,4},{1,9},{9,1},{5,13},{13,5},{2,10},{10,2},... | collective-permute-start | bytes 393224 | tf_op jit(solution)/shard_map/ppermute | solution.py:220
  77.4 7.0 %collective-permute-start.10 = (bf16[512,128]{1,0:T(8,128)(2,1)}, bf16[512,128]{1,0:T(8,128)(2,1)S(1)}, u32[]{:S(2)}, u32[]{:S(2)}) collective-permute-start(bf16[512,128]{1,0:T(8,128)(2,1)} %shard_map.59), channel_id=1, source_target_pairs={{0,12},{12,0},{4,8},{8,4},{1,13},{13,1},{5,9},{9,5},{2,14},{14,2},... | collective-permute-start | bytes 393224 | tf_op jit(solution)/shard_map/ppermute | solution.py:220

commit v3 on v2

--- a/solution.py
+++ b/solution.py
@@ -17,6 +17,7 @@
 BF16 = jnp.bfloat16
 VMEM = pl.BlockSpec(memory_space=pltpu.VMEM)
 SMEM = pl.BlockSpec(memory_space=pltpu.SMEM)
+ANY = pl.BlockSpec(memory_space=pl.ANY)
 HBM = pl.BlockSpec(memory_space=pltpu.HBM)
 LIMIT = 24 << 20
 
@@ -253,7 +254,7 @@
     def held(x):
         return pltpu.with_memory_space_constraint(x, pltpu.VMEM)
 
-    def term(grads, acts_m, acts_e=None):
+    def term(grads, acts_m, acts_e=None, through=None):
         scratch = [pltpu.VMEM((rows, tokens), BF16), pltpu.VMEM((rows, KC), BF16)]
         common = dict(
             out_specs=VMEM,
@@ -264,24 +265,37 @@
         if acts_e is None:
 
             def body(place, g, a, w, c, r, out, grads_t, partial):
-                next_kernel(tile, chunk, place, g, None, a, None, w, c, r, out, None, grads_t, partial)
+                next_kernel(rows // 2, chunk, place, g, None, a, None, w, c, r, out, None, grads_t, partial)
 
             return pl.pallas_call(body, in_specs=[SMEM] + [VMEM] * 5, scratch_shapes=scratch, **common)(
                 place, held(grads), held(acts_m), held(weights), held(col_proj), held(row_proj)
             )
 
-        def body(place, g, a, b, w, c, r, out, chosen, grads_t, partial):
-            next_kernel(tile, chunk, place, g, g, a, b, w, c, r, out, chosen, grads_t, partial)
-
+        def body(place, g, a, b, w, c, r, *refs):
+            out, chosen, grads_t, partial = refs[1 if through is not None else 0], *refs[-3:]
+            next_kernel(rows // 2, chunk, place, g, g, a, b, w, c, r, out, chosen, grads_t, partial)
+
+        operands = (place, held(grads), held(acts_m), held(acts_e), held(weights), held(col_proj), held(row_proj))
+        scratch = [pltpu.VMEM((tokens, depth), BF16)] + scratch
+        if through is None:
+            return pl.pallas_call(body, in_specs=[SMEM] + [VMEM] * 6, scratch_shapes=scratch, **common)(*operands)
+        common["out_specs"] = [VMEM, ANY]
+        common["out_shape"] = [common["out_shape"], jax.ShapeDtypeStruct(through.shape, through.dtype)]
         return pl.pallas_call(
-            body, in_specs=[SMEM] + [VMEM] * 6, scratch_shapes=[pltpu.VMEM((tokens, depth), BF16)] + scratch, **common
-        )(place, held(grads), held(acts_m), held(acts_e), held(weights), held(col_proj), held(row_proj))
+            body,
+            in_specs=[SMEM] + [VMEM] * 6 + [ANY],
+            input_output_aliases={7: 1},
+            scratch_shapes=scratch,
+            **common,
+        )(*operands, through)
 
     near2 = send(near, inner)
     across2 = send(across, outward)
-    near_term = send(term(near_g, near), swap)
+    near_own = term(near_g, near)
     last = send(near2, outward)
-    two_term = send(term(two_g, near2, across2), two)
+    two_own, near_own = term(two_g, near2, across2, near_own)
+    two_term = send(two_own, two)
+    near_term = send(near_own, swap)
     three_term = send(term(three_g, across, last), three)
     sketch = own + near_term.astype(F32) + two_term.astype(F32) + three_term.astype(F32)
     return sketch[None]

time: 85.4 us -> 81.4 us (0.953)
  starting transfers between devices: 21.4 us -> 19.1 us
  Pallas kernels: 55.7 us -> 54.1 us
    ppermute x11, starting transfers between devices: 21.4 us -> 19.1 us  [send(): return lax.ppermute(x, 'blk', pairs)]
    pallas_call x2, Pallas kernels: 24 us -> 22.9 us  [the longest x1 11.6 us: term(): pl.pallas_call(body, in_specs=[SMEM] + [VMEM] * 6 + [ANY], input_output_a...]
  transfers between devices with their start and end apart: 11 -> 11, of which waited for: 1 -> 1; matrix products, arithmetic and copies ran while one was open for 0% -> 0% of each run, Pallas kernels for 65% -> 67%
where the time goes in v3:
time: 81.4 us; the launch traced here: 81.2 us
  Pallas kernels  54.1 us (66%)
  starting transfers between devices  19.1 us (23%)
  waiting for transfers between devices  5.64 us (7%)
    ppermute x11, starting transfers between devices, send(): return lax.ppermute(x, 'blk', pairs)  19.1 us
    pallas_call x1, Pallas kernels, line_shards(): pl.pallas_call(functools.partial(first_kernel, tile, chunk), in_specs=[SM...  16.4 us
    pallas_call x1, Pallas kernels, term(): pl.pallas_call(body, in_specs=[SMEM] + [VMEM] * 5, scratch_shapes=scratch...  12.4 us
    pallas_call x1, Pallas kernels, term(): pl.pallas_call(body, in_specs=[SMEM] + [VMEM] * 6 + [ANY], input_output_a...  11.6 us
    pallas_call x1, Pallas kernels, term(): pl.pallas_call(body, in_specs=[SMEM] + [VMEM] * 6, scratch_shapes=scratch...  11.4 us
    ppermute x11, waiting for transfers between devices, send(): return lax.ppermute(x, 'blk', pairs)  5.64 us
    pallas_call x1, Pallas kernels, line_shards(): pl.pallas_call(split_kernel, in_specs=[SMEM, SMEM, VMEM], out_specs=[VMEM...  2.4 us
  transfers between devices with their start and end apart: 11, of which 1 were waited for; matrix products, arithmetic and copies ran while one was open for 0% of the time, Pallas kernels for 67%

profile of v3, /device:TPU:0, one launch (start us, length us, event | category | flops | bytes accessed | tf_op | source)
XLA Modules:
  0.0 81.2 jit_solution(1667762131363087779)
XLA Ops:
  0.0 3.0 %collective-permute-start.1 = (bf16[48,5120]{1,0:T(8,128)(2,1)}, bf16[48,5120]{1,0:T(8,128)(2,1)}, u32[]{:S(2)}, u32[]{:S(2)}) collective-permute-start(bf16[48,5120]{1,0:T(8,128)(2,1)} %bitcast.6), channel_id=1, source_target_pairs={{0,4},{4,0},{8,12},{12,8},{1,5},{5,1},{9,13},{13,9},{2,6},{6,2},{1... | collective-permute-start | bytes 1474568 | tf_op jit(solution)/shard_map/ppermute | solution.py:221
  3.0 0.7 collective-permute-start.3
  4.4 2.4 %shard_map.55 = (bf16[48,1728]{1,0:T(8,128)(2,1)}, bf16[48,1728]{1,0:T(8,128)(2,1)}, bf16[48,1728]{1,0:T(8,128)(2,1)}, bf16[48,1728]{1,0:T(8,128)(2,1)}) custom-call(s32[1]{0:T(128)S(6)} %copy.8.counts, s32[1]{0:T(128)} %bitcast.place, bf16[48,6912]{1,0:T(8,128)(2,1)} %bitcast.5), custom_call_target="tpu_custom_call" | custom-call | tf_op jit(solution)/shard_map/pallas_call | solution.py:225
  6.8 4.4 %collective-permute-start.5 = (bf16[48,1728]{1,0:T(8,128)(2,1)}, bf16[48,1728]{1,0:T(8,128)(2,1)S(1)}, u32[]{:S(2)}, u32[]{:S(2)}) collective-permute-start(bf16[48,1728]{1,0:T(8,128)(2,1)} %get-tuple-element.21), channel_id=1, source_target_pairs={{0,4},{4,0},{8,12},{12,8},{1,5},{5,1},{9,13},{13,9},{2,6},{6,2},{1... | collective-permute-start | bytes 497672 | tf_op jit(solution)/shard_map/ppermute | solution.py:221
  11.1 0.0 collective-permute-start
  11.1 2.4 %collective-permute-start.8 = (bf16[48,1728]{1,0:T(8,128)(2,1)}, bf16[48,1728]{1,0:T(8,128)(2,1)S(1)}, u32[]{:S(2)}, u32[]{:S(2)}) collective-permute-start(bf16[48,1728]{1,0:T(8,128)(2,1)} %get-tuple-element.24), channel_id=1, source_target_pairs={{0,12},{12,0},{4,8},{8,4},{1,13},{13,1},{5,9},{9,5},{2,14},{14,2},... | collective-permute-start | bytes 497672 | tf_op jit(solution)/shard_map/ppermute | solution.py:221
  13.5 16.4 %shard_map.56 = (f32[512,128]{1,0:T(8,128)}, f32[1728,5120]{1,0:T(8,128)S(1)}, bf16[5120,128]{1,0:T(8,128)(2,1)S(1)}, bf16[512,1728]{1,0:T(8,128)(2,1)S(1)}) custom-call(s32[2]{0:T(128)} %seeds.1, s32[1]{0:T(128)} %bitcast.place, bf16[48,1728]{1,0:T(8,128)(2,1)} %get-tuple-element.15.grads, bf16[48,5120]{1,0:T(8,128)(2,1)} %bitcast.8, f32[1728,5120]{1,0:T(8,128)} %moment.1), custom_call_target="tpu_custom_call" | custom-call | flops 9059696640 | bytes 35389440 | tf_op jit(solution)/shard_map/pallas_call | solution.py:235
  29.9 0.0 collective-permute-done.1.a
  29.9 0.7 collective-permute-start.2
  30.6 0.0 collective-permute-done.3.a
  30.6 1.3 %collective-permute-start.4 = (bf16[48,5120]{1,0:T(8,128)(2,1)S(1)}, bf16[48,5120]{1,0:T(8,128)(2,1)S(1)}, u32[]{:S(2)}, u32[]{:S(2)}) collective-permute-start(bf16[48,5120]{1,0:T(8,128)(2,1)S(1)} %collective-permute-done.3.a), channel_id=1, source_target_pairs={{8,12},{4,0},{9,13},{5,1},{10,14},{6,2},{11,15},{7,3},{24,28},{20,... | collective-permute-start | bytes 1474568 | tf_op jit(solution)/shard_map/ppermute | solution.py:221
  31.9 0.8 copy-done
  32.7 0.0 collective-permute-done.5.g
  32.7 12.4 %shard_map.57.refs_0_ = bf16[512,128]{1,0:T(8,128)(2,1)} custom-call(s32[1]{0:T(128)} %bitcast.place, bf16[48,1728]{1,0:T(8,128)(2,1)S(1)} %collective-permute-done.5.g, bf16[48,5120]{1,0:T(8,128)(2,1)} %collective-permute-done.1.a, f32[1728,5120]{1,0:T(8,128)S(1)} %get-tuple-element.18.w, bf16[5120,128]{1,0:T(8,128)(2,1)S(1)} %get-tuple-element.19.c, ...), custom_call_target="tpu_custom_call" | custom-call | flops 9059696640 | bytes 35389440 | tf_op jit(solution)/shard_map/pallas_call | solution.py:270
  45.1 0.0 collective-permute-done.2.a
  45.1 1.4 %collective-permute-start.9 = (bf16[48,5120]{1,0:T(8,128)(2,1)S(1)}, bf16[48,5120]{1,0:T(8,128)(2,1)S(1)}, u32[]{:S(2)}, u32[]{:S(2)}) collective-permute-start(bf16[48,5120]{1,0:T(8,128)(2,1)S(1)} %collective-permute-done.2.a), channel_id=1, source_target_pairs={{8,12},{4,0},{9,13},{5,1},{10,14},{6,2},{11,15},{7,3},{24,28},{20,... | collective-permute-start | bytes 1474568 | tf_op jit(solution)/shard_map/ppermute | solution.py:221
  46.5 0.0 collective-permute-done.4.b
  46.6 11.6 %shard_map.58 = (bf16[512,128]{1,0:T(8,128)(2,1)}, bf16[512,128]{1,0:T(8,128)(2,1)}) custom-call(s32[1]{0:T(128)} %bitcast.place, bf16[48,1728]{1,0:T(8,128)(2,1)S(1)} %collective-permute-done.g, bf16[48,5120]{1,0:T(8,128)(2,1)S(1)} %collective-permute-done.2.a, bf16[48,5120]{1,0:T(8,128)(2,1)S(1)} %collective-permute-done.4.b, ...), custom_call_target="tpu_custom_call", output_to_operand_aliasing={{1}: (7, {})} | custom-call | flops 9059696640 | bytes 35389440 | tf_op jit(solution)/shard_map/pallas_call | solution.py:284
  58.1 2.7 %collective-permute-start.6 = (bf16[512,128]{1,0:T(8,128)(2,1)}, bf16[512,128]{1,0:T(8,128)(2,1)S(1)}, u32[]{:S(2)}, u32[]{:S(2)}) collective-permute-start(bf16[512,128]{1,0:T(8,128)(2,1)} %get-tuple-element.22), channel_id=1, source_target_pairs={{0,4},{4,0},{8,12},{12,8},{1,5},{5,1},{9,13},{13,9},{2,6},{6,2},{1... | collective-permute-start | bytes 393224 | tf_op jit(solution)/shard_map/ppermute | solution.py:221
  60.8 1.2 %collective-permute-start.7 = (bf16[512,128]{1,0:T(8,128)(2,1)}, bf16[512,128]{1,0:T(8,128)(2,1)S(1)}, u32[]{:S(2)}, u32[]{:S(2)}) collective-permute-start(bf16[512,128]{1,0:T(8,128)(2,1)} %get-tuple-element.23), channel_id=1, source_target_pairs={{0,8},{8,0},{4,12},{12,4},{1,9},{9,1},{5,13},{13,5},{2,10},{10,2},... | collective-permute-start | bytes 393224 | tf_op jit(solution)/shard_map/ppermute | solution.py:221
  62.0 11.4 %shard_map.59 = bf16[512,128]{1,0:T(8,128)(2,1)} custom-call(s32[1]{0:T(128)} %bitcast.place, bf16[48,1728]{1,0:T(8,128)(2,1)S(1)} %collective-permute-done.8.g, bf16[48,5120]{1,0:T(8,128)(2,1)S(1)} %copy-done.1, bf16[48,5120]{1,0:T(8,128)(2,1)S(1)} %collective-permute-done.9.b, f32[1728,5120]{1,0:T(8,128)S(1)} %get-tuple-element.18.w, ...), custom_call_target="tpu_custom_call" | custom-call | flops 9059696640 | bytes 35389440 | tf_op jit(solution)/shard_map/pallas_call | solution.py:281
  73.3 1.5 %collective-permute-start.10 = (bf16[512,128]{1,0:T(8,128)(2,1)}, bf16[512,128]{1,0:T(8,128)(2,1)S(1)}, u32[]{:S(2)}, u32[]{:S(2)}) collective-permute-start(bf16[512,128]{1,0:T(8,128)(2,1)} %shard_map.59), channel_id=1, source_target_pairs={{0,12},{12,0},{4,8},{8,4},{1,13},{13,1},{5,9},{9,5},{2,14},{14,2},... | collective-permute-start | bytes 393224 | tf_op jit(solution)/shard_map/ppermute | solution.py:221
  74.8 5.6 %collective-permute-done.10 = bf16[512,128]{1,0:T(8,128)(2,1)S(1)} collective-permute-done((bf16[512,128]{1,0:T(8,128)(2,1)}, bf16[512,128]{1,0:T(8,128)(2,1)S(1)}, u32[]{:S(2)}, u32[]{:S(2)}) %collective-permute-start.10) | collective-permute-done | bytes 131104 | tf_op jit(solution)/shard_map/ppermute | solution.py:221
  80.4 0.8 add_bitcast_fusion
  (10 shorter events, 0.0 us)
Async XLA Ops:
  0.0 29.9 %collective-permute-start.1 = (bf16[48,5120]{1,0:T(8,128)(2,1)}, bf16[48,5120]{1,0:T(8,128)(2,1)}, u32[]{:S(2)}, u32[]{:S(2)}) collective-permute-start(bf16[48,5120]{1,0:T(8,128)(2,1)} %bitcast.6), channel_id=1, source_target_pairs={{0,4},{4,0},{8,12},{12,8},{1,5},{5,1},{9,13},{13,9},{2,6},{6,2},{1... | collective-permute-start | bytes 1474568 | tf_op jit(solution)/shard_map/ppermute | solution.py:221
  3.0 27.6 %collective-permute-start.3 = (bf16[48,5120]{1,0:T(8,128)(2,1)}, bf16[48,5120]{1,0:T(8,128)(2,1)S(1)}, u32[]{:S(2)}, u32[]{:S(2)}) collective-permute-start(bf16[48,5120]{1,0:T(8,128)(2,1)} %bitcast.7), channel_id=1, source_target_pairs={{4,8},{8,4},{5,9},{9,5},{6,10},{10,6},{7,11},{11,7},{20,24},{24,20... | collective-permute-start | bytes 1474568 | tf_op jit(solution)/shard_map/ppermute | solution.py:221
  6.8 25.9 %collective-permute-start.5 = (bf16[48,1728]{1,0:T(8,128)(2,1)}, bf16[48,1728]{1,0:T(8,128)(2,1)S(1)}, u32[]{:S(2)}, u32[]{:S(2)}) collective-permute-start(bf16[48,1728]{1,0:T(8,128)(2,1)} %get-tuple-element.21), channel_id=1, source_target_pairs={{0,4},{4,0},{8,12},{12,8},{1,5},{5,1},{9,13},{13,9},{2,6},{6,2},{1... | collective-permute-start | bytes 497672 | tf_op jit(solution)/shard_map/ppermute | solution.py:221
  11.1 35.4 %collective-permute-start = (bf16[48,1728]{1,0:T(8,128)(2,1)}, bf16[48,1728]{1,0:T(8,128)(2,1)S(1)}, u32[]{:S(2)}, u32[]{:S(2)}) collective-permute-start(bf16[48,1728]{1,0:T(8,128)(2,1)} %get-tuple-element.17), channel_id=1, source_target_pairs={{0,8},{8,0},{4,12},{12,4},{1,9},{9,1},{5,13},{13,5},{2,10},{10,2},... | collective-permute-start | bytes 497672 | tf_op jit(solution)/shard_map/ppermute | solution.py:221
  11.1 50.8 %collective-permute-start.8 = (bf16[48,1728]{1,0:T(8,128)(2,1)}, bf16[48,1728]{1,0:T(8,128)(2,1)S(1)}, u32[]{:S(2)}, u32[]{:S(2)}) collective-permute-start(bf16[48,1728]{1,0:T(8,128)(2,1)} %get-tuple-element.24), channel_id=1, source_target_pairs={{0,12},{12,0},{4,8},{8,4},{1,13},{13,1},{5,9},{9,5},{2,14},{14,2},... | collective-permute-start | bytes 497672 | tf_op jit(solution)/shard_map/ppermute | solution.py:221
  29.9 15.2 %collective-permute-start.2 = (bf16[48,5120]{1,0:T(8,128)(2,1)}, bf16[48,5120]{1,0:T(8,128)(2,1)S(1)}, u32[]{:S(2)}, u32[]{:S(2)}) collective-permute-start(bf16[48,5120]{1,0:T(8,128)(2,1)} %collective-permute-done.1.a), channel_id=1, source_target_pairs={{4,8},{8,4},{5,9},{9,5},{6,10},{10,6},{7,11},{11,7},{20,24},{24,20... | collective-permute-start | bytes 1474568 | tf_op jit(solution)/shard_map/ppermute | solution.py:221
  30.6 15.9 %collective-permute-start.4 = (bf16[48,5120]{1,0:T(8,128)(2,1)S(1)}, bf16[48,5120]{1,0:T(8,128)(2,1)S(1)}, u32[]{:S(2)}, u32[]{:S(2)}) collective-permute-start(bf16[48,5120]{1,0:T(8,128)(2,1)S(1)} %collective-permute-done.3.a), channel_id=1, source_target_pairs={{8,12},{4,0},{9,13},{5,1},{10,14},{6,2},{11,15},{7,3},{24,28},{20,... | collective-permute-start | bytes 1474568 | tf_op jit(solution)/shard_map/ppermute | solution.py:221
  31.9 0.8 copy-start
  32.7 29.3 %copy-start.1 = (bf16[48,5120]{1,0:T(8,128)(2,1)S(1)}, bf16[48,5120]{1,0:T(8,128)(2,1)}, u32[]{:S(2)}) copy-start(bf16[48,5120]{1,0:T(8,128)(2,1)} %copy-done) | copy-start | bytes 1474564
  45.1 35.3 %copy-start.2 = (f32[512,128]{1,0:T(8,128)S(1)}, f32[512,128]{1,0:T(8,128)}, u32[]{:S(2)}) copy-start(f32[512,128]{1,0:T(8,128)} %get-tuple-element.16) | copy-start | bytes 786436
  45.1 16.8 %collective-permute-start.9 = (bf16[48,5120]{1,0:T(8,128)(2,1)S(1)}, bf16[48,5120]{1,0:T(8,128)(2,1)S(1)}, u32[]{:S(2)}, u32[]{:S(2)}) collective-permute-start(bf16[48,5120]{1,0:T(8,128)(2,1)S(1)} %collective-permute-done.2.a), channel_id=1, source_target_pairs={{8,12},{4,0},{9,13},{5,1},{10,14},{6,2},{11,15},{7,3},{24,28},{20,... | collective-permute-start | bytes 1474568 | tf_op jit(solution)/shard_map/ppermute | solution.py:221
  58.1 16.7 %collective-permute-start.6 = (bf16[512,128]{1,0:T(8,128)(2,1)}, bf16[512,128]{1,0:T(8,128)(2,1)S(1)}, u32[]{:S(2)}, u32[]{:S(2)}) collective-permute-start(bf16[512,128]{1,0:T(8,128)(2,1)} %get-tuple-element.22), channel_id=1, source_target_pairs={{0,4},{4,0},{8,12},{12,8},{1,5},{5,1},{9,13},{13,9},{2,6},{6,2},{1... | collective-permute-start | bytes 393224 | tf_op jit(solution)/shard_map/ppermute | solution.py:221
  60.8 14.0 %collective-permute-start.7 = (bf16[512,128]{1,0:T(8,128)(2,1)}, bf16[512,128]{1,0:T(8,128)(2,1)S(1)}, u32[]{:S(2)}, u32[]{:S(2)}) collective-permute-start(bf16[512,128]{1,0:T(8,128)(2,1)} %get-tuple-element.23), channel_id=1, source_target_pairs={{0,8},{8,0},{4,12},{12,4},{1,9},{9,1},{5,13},{13,5},{2,10},{10,2},... | collective-permute-start | bytes 393224 | tf_op jit(solution)/shard_map/ppermute | solution.py:221
  73.3 7.1 %collective-permute-start.10 = (bf16[512,128]{1,0:T(8,128)(2,1)}, bf16[512,128]{1,0:T(8,128)(2,1)S(1)}, u32[]{:S(2)}, u32[]{:S(2)}) collective-permute-start(bf16[512,128]{1,0:T(8,128)(2,1)} %shard_map.59), channel_id=1, source_target_pairs={{0,12},{12,0},{4,8},{8,4},{1,13},{13,1},{5,9},{9,5},{2,14},{14,2},... | collective-permute-start | bytes 393224 | tf_op jit(solution)/shard_map/ppermute | solution.py:221

commit v4 on v3

--- a/solution.py
+++ b/solution.py
@@ -167,7 +167,7 @@
     project_rows(row_proj, partial, out)
 
 
-def next_kernel(tile, chunk, place, grads_m, grads_e, acts_m, acts_e, weights, col_proj, row_proj, out, acts, grads_t, partial):
+def next_kernel(tile, chunk, place, grads_m, grads_e, acts_m, acts_e, weights, col_proj, row_proj, out, acts, grads_t, partial, far=False):
     rows, depth = weights.shape
     tiles = rows // tile
     if grads_e is None:
@@ -178,7 +178,10 @@
 
         @pl.when(middle)
         def _():
-            acts[...] = acts_m[...]
+            if far:
+                pltpu.sync_copy(acts_m, acts)
+            else:
+                acts[...] = acts_m[...]
 
         @pl.when(jnp.logical_not(middle))
         def _():
@@ -273,12 +276,14 @@
 
         def body(place, g, a, b, w, c, r, *refs):
             out, chosen, grads_t, partial = refs[1 if through is not None else 0], *refs[-3:]
-            next_kernel(rows // 2, chunk, place, g, g, a, b, w, c, r, out, chosen, grads_t, partial)
-
-        operands = (place, held(grads), held(acts_m), held(acts_e), held(weights), held(col_proj), held(row_proj))
+            next_kernel(rows // 2, chunk, place, g, g, a, b, w, c, r, out, chosen, grads_t, partial, through is None)
+
+        operands = (place, held(grads), acts_m if through is None else held(acts_m), held(acts_e), held(weights), held(col_proj), held(row_proj))
         scratch = [pltpu.VMEM((tokens, depth), BF16)] + scratch
         if through is None:
-            return pl.pallas_call(body, in_specs=[SMEM] + [VMEM] * 6, scratch_shapes=scratch, **common)(*operands)
+            return pl.pallas_call(
+                body, in_specs=[SMEM, VMEM, ANY] + [VMEM] * 4, scratch_shapes=scratch, **common
+            )(*operands)
         common["out_specs"] = [VMEM, ANY]
         common["out_shape"] = [common["out_shape"], jax.ShapeDtypeStruct(through.shape, through.dtype)]
         return pl.pallas_call(

time: 81.4 us -> 79.6 us (0.978)
  Pallas kernels: 54.1 us -> 53 us
    pallas_call x1, Pallas kernels: 12.4 us -> 11.3 us  [term(): pl.pallas_call(body, in_specs=[SMEM] + [VMEM] * 5, scratch_shapes=scratch...]
where the time goes in v4:
time: 79.6 us; the launch traced here: 79.3 us
  Pallas kernels  53 us (67%)
  starting transfers between devices  19.2 us (24%)
  waiting for transfers between devices  5.61 us (7%)
    ppermute x11, starting transfers between devices, send(): return lax.ppermute(x, 'blk', pairs)  19.2 us
    pallas_call x1, Pallas kernels, line_shards(): pl.pallas_call(functools.partial(first_kernel, tile, chunk), in_specs=[SM...  16.4 us
    pallas_call x1, Pallas kernels, term(): pl.pallas_call(body, in_specs=[SMEM] + [VMEM] * 6 + [ANY], input_output_a...  11.6 us
    pallas_call x1, Pallas kernels, term(): pl.pallas_call(body, in_specs=[SMEM, VMEM, ANY] + [VMEM] * 4, scratch_sha...  11.4 us
    pallas_call x1, Pallas kernels, term(): pl.pallas_call(body, in_specs=[SMEM] + [VMEM] * 5, scratch_shapes=scratch...  11.3 us
    ppermute x11, waiting for transfers between devices, send(): return lax.ppermute(x, 'blk', pairs)  5.61 us
    pallas_call x1, Pallas kernels, line_shards(): pl.pallas_call(split_kernel, in_specs=[SMEM, SMEM, VMEM], out_specs=[VMEM...  2.39 us
  transfers between devices with their start and end apart: 11, of which 1 were waited for; matrix products, arithmetic and copies ran while one was open for 0% of the time, Pallas kernels for 67%

profile of v4, /device:TPU:0, one launch (start us, length us, event | category | flops | bytes accessed | tf_op | source)
XLA Modules:
  0.0 79.3 jit_solution(12689835528463677507)
XLA Ops:
  0.0 3.0 %collective-permute-start.1 = (bf16[48,5120]{1,0:T(8,128)(2,1)}, bf16[48,5120]{1,0:T(8,128)(2,1)S(1)}, u32[]{:S(2)}, u32[]{:S(2)}) collective-permute-start(bf16[48,5120]{1,0:T(8,128)(2,1)} %bitcast.6), channel_id=1, source_target_pairs={{0,4},{4,0},{8,12},{12,8},{1,5},{5,1},{9,13},{13,9},{2,6},{6,2},{1... | collective-permute-start | bytes 1474568 | tf_op jit(solution)/shard_map/ppermute | solution.py:224
  3.0 1.4 %collective-permute-start.3 = (bf16[48,5120]{1,0:T(8,128)(2,1)}, bf16[48,5120]{1,0:T(8,128)(2,1)}, u32[]{:S(2)}, u32[]{:S(2)}) collective-permute-start(bf16[48,5120]{1,0:T(8,128)(2,1)} %bitcast.7), channel_id=1, source_target_pairs={{4,8},{8,4},{5,9},{9,5},{6,10},{10,6},{7,11},{11,7},{20,24},{24,20... | collective-permute-start | bytes 1474568 | tf_op jit(solution)/shard_map/ppermute | solution.py:224
  5.1 2.4 %shard_map.55 = (bf16[48,1728]{1,0:T(8,128)(2,1)}, bf16[48,1728]{1,0:T(8,128)(2,1)}, bf16[48,1728]{1,0:T(8,128)(2,1)}, bf16[48,1728]{1,0:T(8,128)(2,1)}) custom-call(s32[1]{0:T(128)S(6)} %copy.8.counts, s32[1]{0:T(128)} %bitcast.place, bf16[48,6912]{1,0:T(8,128)(2,1)} %bitcast.5), custom_call_target="tpu_custom_call" | custom-call | tf_op jit(solution)/shard_map/pallas_call | solution.py:228
  7.5 3.6 %collective-permute-start.5 = (bf16[48,1728]{1,0:T(8,128)(2,1)}, bf16[48,1728]{1,0:T(8,128)(2,1)S(1)}, u32[]{:S(2)}, u32[]{:S(2)}) collective-permute-start(bf16[48,1728]{1,0:T(8,128)(2,1)} %get-tuple-element.21), channel_id=1, source_target_pairs={{0,4},{4,0},{8,12},{12,8},{1,5},{5,1},{9,13},{13,9},{2,6},{6,2},{1... | collective-permute-start | bytes 497672 | tf_op jit(solution)/shard_map/ppermute | solution.py:224
  11.1 0.0 collective-permute-start
  11.1 2.4 %collective-permute-start.8 = (bf16[48,1728]{1,0:T(8,128)(2,1)}, bf16[48,1728]{1,0:T(8,128)(2,1)S(1)}, u32[]{:S(2)}, u32[]{:S(2)}) collective-permute-start(bf16[48,1728]{1,0:T(8,128)(2,1)} %get-tuple-element.24), channel_id=1, source_target_pairs={{0,12},{12,0},{4,8},{8,4},{1,13},{13,1},{5,9},{9,5},{2,14},{14,2},... | collective-permute-start | bytes 497672 | tf_op jit(solution)/shard_map/ppermute | solution.py:224
  13.5 16.4 %shard_map.56 = (f32[512,128]{1,0:T(8,128)}, f32[1728,5120]{1,0:T(8,128)S(1)}, bf16[5120,128]{1,0:T(8,128)(2,1)S(1)}, bf16[512,1728]{1,0:T(8,128)(2,1)S(1)}) custom-call(s32[2]{0:T(128)} %seeds.1, s32[1]{0:T(128)} %bitcast.place, bf16[48,1728]{1,0:T(8,128)(2,1)} %get-tuple-element.15.grads, bf16[48,5120]{1,0:T(8,128)(2,1)} %bitcast.8, f32[1728,5120]{1,0:T(8,128)} %moment.1), custom_call_target="tpu_custom_call" | custom-call | flops 9059696640 | bytes 35389440 | tf_op jit(solution)/shard_map/pallas_call | solution.py:238
  29.9 0.0 collective-permute-done.1.a
  29.9 0.7 collective-permute-start.2
  30.6 0.0 collective-permute-done.3.a
  30.6 1.3 %collective-permute-start.4 = (bf16[48,5120]{1,0:T(8,128)(2,1)}, bf16[48,5120]{1,0:T(8,128)(2,1)S(1)}, u32[]{:S(2)}, u32[]{:S(2)}) collective-permute-start(bf16[48,5120]{1,0:T(8,128)(2,1)} %collective-permute-done.3.a), channel_id=1, source_target_pairs={{8,12},{4,0},{9,13},{5,1},{10,14},{6,2},{11,15},{7,3},{24,28},{20,... | collective-permute-start | bytes 1474568 | tf_op jit(solution)/shard_map/ppermute | solution.py:224
  31.9 11.3 %shard_map.57.refs_0_ = bf16[512,128]{1,0:T(8,128)(2,1)} custom-call(s32[1]{0:T(128)} %bitcast.place, bf16[48,1728]{1,0:T(8,128)(2,1)S(1)} %collective-permute-done.5.g, bf16[48,5120]{1,0:T(8,128)(2,1)S(1)} %collective-permute-done.1.a, f32[1728,5120]{1,0:T(8,128)S(1)} %get-tuple-element.18.w, bf16[5120,128]{1,0:T(8,128)(2,1)S(1)} %get-tuple-element.19.c, ...), custom_call_target="tpu_custom_call" | custom-call | flops 9059696640 | bytes 35389440 | tf_op jit(solution)/shard_map/pallas_call | solution.py:273
  43.2 1.4 %collective-permute-start.9 = (bf16[48,5120]{1,0:T(8,128)(2,1)S(1)}, bf16[48,5120]{1,0:T(8,128)(2,1)S(1)}, u32[]{:S(2)}, u32[]{:S(2)}) collective-permute-start(bf16[48,5120]{1,0:T(8,128)(2,1)S(1)} %collective-permute-done.2.a), channel_id=1, source_target_pairs={{8,12},{4,0},{9,13},{5,1},{10,14},{6,2},{11,15},{7,3},{24,28},{20,... | collective-permute-start | bytes 1474568 | tf_op jit(solution)/shard_map/ppermute | solution.py:224
  44.7 0.0 collective-permute-done.g
  44.7 0.0 collective-permute-done.4.b
  44.7 11.6 %shard_map.58 = (bf16[512,128]{1,0:T(8,128)(2,1)}, bf16[512,128]{1,0:T(8,128)(2,1)}) custom-call(s32[1]{0:T(128)} %bitcast.place, bf16[48,1728]{1,0:T(8,128)(2,1)S(1)} %collective-permute-done.g, bf16[48,5120]{1,0:T(8,128)(2,1)S(1)} %collective-permute-done.2.a, bf16[48,5120]{1,0:T(8,128)(2,1)S(1)} %collective-permute-done.4.b, ...), custom_call_target="tpu_custom_call", output_to_operand_aliasing={{1}: (7, {})} | custom-call | flops 9059696640 | bytes 35389440 | tf_op jit(solution)/shard_map/pallas_call | solution.py:289
  56.2 2.7 %collective-permute-start.6 = (bf16[512,128]{1,0:T(8,128)(2,1)}, bf16[512,128]{1,0:T(8,128)(2,1)S(1)}, u32[]{:S(2)}, u32[]{:S(2)}) collective-permute-start(bf16[512,128]{1,0:T(8,128)(2,1)} %get-tuple-element.22), channel_id=1, source_target_pairs={{0,4},{4,0},{8,12},{12,8},{1,5},{5,1},{9,13},{13,9},{2,6},{6,2},{1... | collective-permute-start | bytes 393224 | tf_op jit(solution)/shard_map/ppermute | solution.py:224
  58.9 1.2 %collective-permute-start.7 = (bf16[512,128]{1,0:T(8,128)(2,1)}, bf16[512,128]{1,0:T(8,128)(2,1)S(1)}, u32[]{:S(2)}, u32[]{:S(2)}) collective-permute-start(bf16[512,128]{1,0:T(8,128)(2,1)} %get-tuple-element.23), channel_id=1, source_target_pairs={{0,8},{8,0},{4,12},{12,4},{1,9},{9,1},{5,13},{13,5},{2,10},{10,2},... | collective-permute-start | bytes 393224 | tf_op jit(solution)/shard_map/ppermute | solution.py:224
  60.1 0.0 collective-permute-done.8.g
  60.1 0.0 collective-permute-done.9.b
  60.1 11.4 %shard_map.59 = bf16[512,128]{1,0:T(8,128)(2,1)} custom-call(s32[1]{0:T(128)} %bitcast.place, bf16[48,1728]{1,0:T(8,128)(2,1)S(1)} %collective-permute-done.8.g, bf16[48,5120]{1,0:T(8,128)(2,1)} %collective-permute-done.3.a, bf16[48,5120]{1,0:T(8,128)(2,1)S(1)} %collective-permute-done.9.b, f32[1728,5120]{1,0:T(8,128)S(1)} %get-tuple-element.18.w, ...), custom_call_target="tpu_custom_call" | custom-call | flops 9059696640 | bytes 35389440 | tf_op jit(solution)/shard_map/pallas_call | solution.py:284
  71.5 1.5 %collective-permute-start.10 = (bf16[512,128]{1,0:T(8,128)(2,1)}, bf16[512,128]{1,0:T(8,128)(2,1)S(1)}, u32[]{:S(2)}, u32[]{:S(2)}) collective-permute-start(bf16[512,128]{1,0:T(8,128)(2,1)} %shard_map.59), channel_id=1, source_target_pairs={{0,12},{12,0},{4,8},{8,4},{1,13},{13,1},{5,9},{9,5},{2,14},{14,2},... | collective-permute-start | bytes 393224 | tf_op jit(solution)/shard_map/ppermute | solution.py:224
  72.9 5.6 %collective-permute-done.10 = bf16[512,128]{1,0:T(8,128)(2,1)S(1)} collective-permute-done((bf16[512,128]{1,0:T(8,128)(2,1)}, bf16[512,128]{1,0:T(8,128)(2,1)S(1)}, u32[]{:S(2)}, u32[]{:S(2)}) %collective-permute-start.10) | collective-permute-done | bytes 131104 | tf_op jit(solution)/shard_map/ppermute | solution.py:224
  78.5 0.8 add_bitcast_fusion
  (6 shorter events, 0.0 us)
Async XLA Ops:
  0.0 29.9 %collective-permute-start.1 = (bf16[48,5120]{1,0:T(8,128)(2,1)}, bf16[48,5120]{1,0:T(8,128)(2,1)S(1)}, u32[]{:S(2)}, u32[]{:S(2)}) collective-permute-start(bf16[48,5120]{1,0:T(8,128)(2,1)} %bitcast.6), channel_id=1, source_target_pairs={{0,4},{4,0},{8,12},{12,8},{1,5},{5,1},{9,13},{13,9},{2,6},{6,2},{1... | collective-permute-start | bytes 1474568 | tf_op jit(solution)/shard_map/ppermute | solution.py:224
  3.0 27.6 %collective-permute-start.3 = (bf16[48,5120]{1,0:T(8,128)(2,1)}, bf16[48,5120]{1,0:T(8,128)(2,1)}, u32[]{:S(2)}, u32[]{:S(2)}) collective-permute-start(bf16[48,5120]{1,0:T(8,128)(2,1)} %bitcast.7), channel_id=1, source_target_pairs={{4,8},{8,4},{5,9},{9,5},{6,10},{10,6},{7,11},{11,7},{20,24},{24,20... | collective-permute-start | bytes 1474568 | tf_op jit(solution)/shard_map/ppermute | solution.py:224
  7.5 24.4 %collective-permute-start.5 = (bf16[48,1728]{1,0:T(8,128)(2,1)}, bf16[48,1728]{1,0:T(8,128)(2,1)S(1)}, u32[]{:S(2)}, u32[]{:S(2)}) collective-permute-start(bf16[48,1728]{1,0:T(8,128)(2,1)} %get-tuple-element.21), channel_id=1, source_target_pairs={{0,4},{4,0},{8,12},{12,8},{1,5},{5,1},{9,13},{13,9},{2,6},{6,2},{1... | collective-permute-start | bytes 497672 | tf_op jit(solution)/shard_map/ppermute | solution.py:224
  11.1 33.5 %collective-permute-start = (bf16[48,1728]{1,0:T(8,128)(2,1)}, bf16[48,1728]{1,0:T(8,128)(2,1)S(1)}, u32[]{:S(2)}, u32[]{:S(2)}) collective-permute-start(bf16[48,1728]{1,0:T(8,128)(2,1)} %get-tuple-element.17), channel_id=1, source_target_pairs={{0,8},{8,0},{4,12},{12,4},{1,9},{9,1},{5,13},{13,5},{2,10},{10,2},... | collective-permute-start | bytes 497672 | tf_op jit(solution)/shard_map/ppermute | solution.py:224
  11.1 49.0 %collective-permute-start.8 = (bf16[48,1728]{1,0:T(8,128)(2,1)}, bf16[48,1728]{1,0:T(8,128)(2,1)S(1)}, u32[]{:S(2)}, u32[]{:S(2)}) collective-permute-start(bf16[48,1728]{1,0:T(8,128)(2,1)} %get-tuple-element.24), channel_id=1, source_target_pairs={{0,12},{12,0},{4,8},{8,4},{1,13},{13,1},{5,9},{9,5},{2,14},{14,2},... | collective-permute-start | bytes 497672 | tf_op jit(solution)/shard_map/ppermute | solution.py:224
  29.9 13.3 %collective-permute-start.2 = (bf16[48,5120]{1,0:T(8,128)(2,1)S(1)}, bf16[48,5120]{1,0:T(8,128)(2,1)S(1)}, u32[]{:S(2)}, u32[]{:S(2)}) collective-permute-start(bf16[48,5120]{1,0:T(8,128)(2,1)S(1)} %collective-permute-done.1.a), channel_id=1, source_target_pairs={{4,8},{8,4},{5,9},{9,5},{6,10},{10,6},{7,11},{11,7},{20,24},{24,20... | collective-permute-start | bytes 1474568 | tf_op jit(solution)/shard_map/ppermute | solution.py:224
  30.6 14.1 %collective-permute-start.4 = (bf16[48,5120]{1,0:T(8,128)(2,1)}, bf16[48,5120]{1,0:T(8,128)(2,1)S(1)}, u32[]{:S(2)}, u32[]{:S(2)}) collective-permute-start(bf16[48,5120]{1,0:T(8,128)(2,1)} %collective-permute-done.3.a), channel_id=1, source_target_pairs={{8,12},{4,0},{9,13},{5,1},{10,14},{6,2},{11,15},{7,3},{24,28},{20,... | collective-permute-start | bytes 1474568 | tf_op jit(solution)/shard_map/ppermute | solution.py:224
  43.2 35.3 %copy-start = (f32[512,128]{1,0:T(8,128)S(1)}, f32[512,128]{1,0:T(8,128)}, u32[]{:S(2)}) copy-start(f32[512,128]{1,0:T(8,128)} %get-tuple-element.16) | copy-start | bytes 786436
  43.2 16.9 %collective-permute-start.9 = (bf16[48,5120]{1,0:T(8,128)(2,1)S(1)}, bf16[48,5120]{1,0:T(8,128)(2,1)S(1)}, u32[]{:S(2)}, u32[]{:S(2)}) collective-permute-start(bf16[48,5120]{1,0:T(8,128)(2,1)S(1)} %collective-permute-done.2.a), channel_id=1, source_target_pairs={{8,12},{4,0},{9,13},{5,1},{10,14},{6,2},{11,15},{7,3},{24,28},{20,... | collective-permute-start | bytes 1474568 | tf_op jit(solution)/shard_map/ppermute | solution.py:224
  56.2 16.7 %collective-permute-start.6 = (bf16[512,128]{1,0:T(8,128)(2,1)}, bf16[512,128]{1,0:T(8,128)(2,1)S(1)}, u32[]{:S(2)}, u32[]{:S(2)}) collective-permute-start(bf16[512,128]{1,0:T(8,128)(2,1)} %get-tuple-element.22), channel_id=1, source_target_pairs={{0,4},{4,0},{8,12},{12,8},{1,5},{5,1},{9,13},{13,9},{2,6},{6,2},{1... | collective-permute-start | bytes 393224 | tf_op jit(solution)/shard_map/ppermute | solution.py:224
  58.9 14.0 %collective-permute-start.7 = (bf16[512,128]{1,0:T(8,128)(2,1)}, bf16[512,128]{1,0:T(8,128)(2,1)S(1)}, u32[]{:S(2)}, u32[]{:S(2)}) collective-permute-start(bf16[512,128]{1,0:T(8,128)(2,1)} %get-tuple-element.23), channel_id=1, source_target_pairs={{0,8},{8,0},{4,12},{12,4},{1,9},{9,1},{5,13},{13,5},{2,10},{10,2},... | collective-permute-start | bytes 393224 | tf_op jit(solution)/shard_map/ppermute | solution.py:224
  71.5 7.1 %collective-permute-start.10 = (bf16[512,128]{1,0:T(8,128)(2,1)}, bf16[512,128]{1,0:T(8,128)(2,1)S(1)}, u32[]{:S(2)}, u32[]{:S(2)}) collective-permute-start(bf16[512,128]{1,0:T(8,128)(2,1)} %shard_map.59), channel_id=1, source_target_pairs={{0,12},{12,0},{4,8},{8,4},{1,13},{13,1},{5,9},{9,5},{2,14},{14,2},... | collective-permute-start | bytes 393224 | tf_op jit(solution)/shard_map/ppermute | solution.py:224

commit v5 on v4

--- a/solution.py
+++ b/solution.py
@@ -189,19 +189,19 @@
 
         grads_t[...] = grads_m[...].astype(F32).T.astype(BF16)
 
-    @pl.loop(0, tiles)
-    def _(t):
-        part = pl.ds(pl.multiple_of(t * tile, 16), tile)
+    cut = -(-(rows // 2) // 128) * 128
+    sketch = jnp.zeros((KR, KC), F32)
+    for begin, end in ((0, cut), (cut, rows)):
+        part = pl.ds(begin, end - begin)
         left = grads_t[part]
-        total = jnp.zeros((tile, KC), F32)
+        total = jnp.zeros((end - begin, KC), F32)
         for c in range(0, depth, chunk):
             cols = pl.ds(c, chunk)
             gradient = jnp.dot(left, acts[:, cols], preferred_element_type=F32)
             scaled = (gradient * weights[part, cols]).astype(BF16)
             total += jnp.dot(scaled, col_proj[cols], preferred_element_type=F32)
-        partial[part] = total.astype(BF16)
-
-    project_rows(row_proj, partial, out)
+        sketch += jnp.dot(row_proj[:, begin:end], total.astype(BF16), preferred_element_type=F32)
+    out[...] = sketch.astype(out.dtype)
 
 
 def line_shards(acts, outgrads, moment, counts, seeds):

time: 79.6 us -> 78.6 us (0.987)
  Pallas kernels: 53 us -> 51.8 us
  transfers between devices with their start and end apart: 11 -> 11, of which waited for: 1 -> 2; matrix products, arithmetic and copies ran while one was open for 0% -> 0% of each run, Pallas kernels for 67% -> 66%
where the time goes in v5:
time: 78.6 us; the launch traced here: 78.3 us
  Pallas kernels  51.8 us (66%)
  starting transfers between devices  19.2 us (24%)
  waiting for transfers between devices  5.81 us (7%)
    ppermute x11, starting transfers between devices, send(): return lax.ppermute(x, 'blk', pairs)  19.2 us
    pallas_call x1, Pallas kernels, line_shards(): pl.pallas_call(functools.partial(first_kernel, tile, chunk), in_specs=[SM...  16.4 us
    pallas_call x1, Pallas kernels, term(): pl.pallas_call(body, in_specs=[SMEM, VMEM, ANY] + [VMEM] * 4, scratch_sha...  11.1 us
    pallas_call x1, Pallas kernels, term(): pl.pallas_call(body, in_specs=[SMEM] + [VMEM] * 6 + [ANY], input_output_a...  11.1 us
    pallas_call x1, Pallas kernels, term(): pl.pallas_call(body, in_specs=[SMEM] + [VMEM] * 5, scratch_shapes=scratch...  10.8 us
    ppermute x11, waiting for transfers between devices, send(): return lax.ppermute(x, 'blk', pairs)  5.81 us
    pallas_call x1, Pallas kernels, line_shards(): pl.pallas_call(split_kernel, in_specs=[SMEM, SMEM, VMEM], out_specs=[VMEM...  2.39 us
  transfers between devices with their start and end apart: 11, of which 2 were waited for; matrix products, arithmetic and copies ran while one was open for 0% of the time, Pallas kernels for 66%

profile of v5, /device:TPU:0, one launch (start us, length us, event | category | flops | bytes accessed | tf_op | source)
XLA Modules:
  0.0 78.3 jit_solution(17707434961908642838)
XLA Ops:
  0.0 3.0 %collective-permute-start.1 = (bf16[48,5120]{1,0:T(8,128)(2,1)}, bf16[48,5120]{1,0:T(8,128)(2,1)S(1)}, u32[]{:S(2)}, u32[]{:S(2)}) collective-permute-start(bf16[48,5120]{1,0:T(8,128)(2,1)} %bitcast.6), channel_id=1, source_target_pairs={{0,4},{4,0},{8,12},{12,8},{1,5},{5,1},{9,13},{13,9},{2,6},{6,2},{1... | collective-permute-start | bytes 1474568 | tf_op jit(solution)/shard_map/ppermute | solution.py:224
  3.0 1.4 %collective-permute-start.3 = (bf16[48,5120]{1,0:T(8,128)(2,1)}, bf16[48,5120]{1,0:T(8,128)(2,1)}, u32[]{:S(2)}, u32[]{:S(2)}) collective-permute-start(bf16[48,5120]{1,0:T(8,128)(2,1)} %bitcast.7), channel_id=1, source_target_pairs={{4,8},{8,4},{5,9},{9,5},{6,10},{10,6},{7,11},{11,7},{20,24},{24,20... | collective-permute-start | bytes 1474568 | tf_op jit(solution)/shard_map/ppermute | solution.py:224
  5.1 2.4 %shard_map.55 = (bf16[48,1728]{1,0:T(8,128)(2,1)}, bf16[48,1728]{1,0:T(8,128)(2,1)}, bf16[48,1728]{1,0:T(8,128)(2,1)}, bf16[48,1728]{1,0:T(8,128)(2,1)}) custom-call(s32[1]{0:T(128)S(6)} %copy.8.counts, s32[1]{0:T(128)} %bitcast.place, bf16[48,6912]{1,0:T(8,128)(2,1)} %bitcast.5), custom_call_target="tpu_custom_call" | custom-call | tf_op jit(solution)/shard_map/pallas_call | solution.py:228
  7.5 3.6 %collective-permute-start.5 = (bf16[48,1728]{1,0:T(8,128)(2,1)}, bf16[48,1728]{1,0:T(8,128)(2,1)S(1)}, u32[]{:S(2)}, u32[]{:S(2)}) collective-permute-start(bf16[48,1728]{1,0:T(8,128)(2,1)} %get-tuple-element.21), channel_id=1, source_target_pairs={{0,4},{4,0},{8,12},{12,8},{1,5},{5,1},{9,13},{13,9},{2,6},{6,2},{1... | collective-permute-start | bytes 497672 | tf_op jit(solution)/shard_map/ppermute | solution.py:224
  11.1 2.4 %collective-permute-start.8 = (bf16[48,1728]{1,0:T(8,128)(2,1)}, bf16[48,1728]{1,0:T(8,128)(2,1)S(1)}, u32[]{:S(2)}, u32[]{:S(2)}) collective-permute-start(bf16[48,1728]{1,0:T(8,128)(2,1)} %get-tuple-element.24), channel_id=1, source_target_pairs={{0,12},{12,0},{4,8},{8,4},{1,13},{13,1},{5,9},{9,5},{2,14},{14,2},... | collective-permute-start | bytes 497672 | tf_op jit(solution)/shard_map/ppermute | solution.py:224
  13.5 16.4 %shard_map.56 = (f32[512,128]{1,0:T(8,128)}, f32[1728,5120]{1,0:T(8,128)S(1)}, bf16[5120,128]{1,0:T(8,128)(2,1)S(1)}, bf16[512,1728]{1,0:T(8,128)(2,1)S(1)}) custom-call(s32[2]{0:T(128)} %seeds.1, s32[1]{0:T(128)} %bitcast.place, bf16[48,1728]{1,0:T(8,128)(2,1)} %get-tuple-element.15.grads, bf16[48,5120]{1,0:T(8,128)(2,1)} %bitcast.8, f32[1728,5120]{1,0:T(8,128)} %moment.1), custom_call_target="tpu_custom_call" | custom-call | flops 9059696640 | bytes 35389440 | tf_op jit(solution)/shard_map/pallas_call | solution.py:238
  29.9 0.0 collective-permute-done.1.a
  29.9 0.7 collective-permute-start.2
  30.6 1.5 %collective-permute-start.4 = (bf16[48,5120]{1,0:T(8,128)(2,1)}, bf16[48,5120]{1,0:T(8,128)(2,1)S(1)}, u32[]{:S(2)}, u32[]{:S(2)}) collective-permute-start(bf16[48,5120]{1,0:T(8,128)(2,1)} %collective-permute-done.3.a), channel_id=1, source_target_pairs={{8,12},{4,0},{9,13},{5,1},{10,14},{6,2},{11,15},{7,3},{24,28},{20,... | collective-permute-start | bytes 1474568 | tf_op jit(solution)/shard_map/ppermute | solution.py:224
  32.1 0.0 collective-permute-done.5.g
  32.1 10.8 %shard_map.57.refs_0_ = bf16[512,128]{1,0:T(8,128)(2,1)} custom-call(s32[1]{0:T(128)} %bitcast.place, bf16[48,1728]{1,0:T(8,128)(2,1)S(1)} %collective-permute-done.5.g, bf16[48,5120]{1,0:T(8,128)(2,1)S(1)} %collective-permute-done.1.a, f32[1728,5120]{1,0:T(8,128)S(1)} %get-tuple-element.18.w, bf16[5120,128]{1,0:T(8,128)(2,1)S(1)} %get-tuple-element.19.c, ...), custom_call_target="tpu_custom_call" | custom-call | flops 9059696640 | bytes 35389440 | tf_op jit(solution)/shard_map/pallas_call | solution.py:273
  42.9 0.0 collective-permute-done.2.a
  42.9 1.4 %collective-permute-start.9 = (bf16[48,5120]{1,0:T(8,128)(2,1)S(1)}, bf16[48,5120]{1,0:T(8,128)(2,1)S(1)}, u32[]{:S(2)}, u32[]{:S(2)}) collective-permute-start(bf16[48,5120]{1,0:T(8,128)(2,1)S(1)} %collective-permute-done.2.a), channel_id=1, source_target_pairs={{8,12},{4,0},{9,13},{5,1},{10,14},{6,2},{11,15},{7,3},{24,28},{20,... | collective-permute-start | bytes 1474568 | tf_op jit(solution)/shard_map/ppermute | solution.py:224
  44.4 0.2 collective-permute-done.4.b
  44.6 11.1 %shard_map.58 = (bf16[512,128]{1,0:T(8,128)(2,1)}, bf16[512,128]{1,0:T(8,128)(2,1)}) custom-call(s32[1]{0:T(128)} %bitcast.place, bf16[48,1728]{1,0:T(8,128)(2,1)S(1)} %collective-permute-done.g, bf16[48,5120]{1,0:T(8,128)(2,1)S(1)} %collective-permute-done.2.a, bf16[48,5120]{1,0:T(8,128)(2,1)S(1)} %collective-permute-done.4.b, ...), custom_call_target="tpu_custom_call", output_to_operand_aliasing={{1}: (7, {})} | custom-call | flops 9059696640 | bytes 35389440 | tf_op jit(solution)/shard_map/pallas_call | solution.py:289
  55.7 2.5 %collective-permute-start.6 = (bf16[512,128]{1,0:T(8,128)(2,1)}, bf16[512,128]{1,0:T(8,128)(2,1)S(1)}, u32[]{:S(2)}, u32[]{:S(2)}) collective-permute-start(bf16[512,128]{1,0:T(8,128)(2,1)} %get-tuple-element.22), channel_id=1, source_target_pairs={{0,4},{4,0},{8,12},{12,8},{1,5},{5,1},{9,13},{13,9},{2,6},{6,2},{1... | collective-permute-start | bytes 393224 | tf_op jit(solution)/shard_map/ppermute | solution.py:224
  58.2 1.2 %collective-permute-start.7 = (bf16[512,128]{1,0:T(8,128)(2,1)}, bf16[512,128]{1,0:T(8,128)(2,1)S(1)}, u32[]{:S(2)}, u32[]{:S(2)}) collective-permute-start(bf16[512,128]{1,0:T(8,128)(2,1)} %get-tuple-element.23), channel_id=1, source_target_pairs={{0,8},{8,0},{4,12},{12,4},{1,9},{9,1},{5,13},{13,5},{2,10},{10,2},... | collective-permute-start | bytes 393224 | tf_op jit(solution)/shard_map/ppermute | solution.py:224
  59.3 0.0 collective-permute-done.8.g
  59.3 0.0 collective-permute-done.9.b
  59.4 11.1 %shard_map.59 = bf16[512,128]{1,0:T(8,128)(2,1)} custom-call(s32[1]{0:T(128)} %bitcast.place, bf16[48,1728]{1,0:T(8,128)(2,1)S(1)} %collective-permute-done.8.g, bf16[48,5120]{1,0:T(8,128)(2,1)} %collective-permute-done.3.a, bf16[48,5120]{1,0:T(8,128)(2,1)S(1)} %collective-permute-done.9.b, f32[1728,5120]{1,0:T(8,128)S(1)} %get-tuple-element.18.w, ...), custom_call_target="tpu_custom_call" | custom-call | flops 9059696640 | bytes 35389440 | tf_op jit(solution)/shard_map/pallas_call | solution.py:284
  70.5 1.5 %collective-permute-start.10 = (bf16[512,128]{1,0:T(8,128)(2,1)}, bf16[512,128]{1,0:T(8,128)(2,1)S(1)}, u32[]{:S(2)}, u32[]{:S(2)}) collective-permute-start(bf16[512,128]{1,0:T(8,128)(2,1)} %shard_map.59), channel_id=1, source_target_pairs={{0,12},{12,0},{4,8},{8,4},{1,13},{13,1},{5,9},{9,5},{2,14},{14,2},... | collective-permute-start | bytes 393224 | tf_op jit(solution)/shard_map/ppermute | solution.py:224
  72.0 0.0 collective-permute-done.6
  72.0 5.6 %collective-permute-done.10 = bf16[512,128]{1,0:T(8,128)(2,1)S(1)} collective-permute-done((bf16[512,128]{1,0:T(8,128)(2,1)}, bf16[512,128]{1,0:T(8,128)(2,1)S(1)}, u32[]{:S(2)}, u32[]{:S(2)}) %collective-permute-start.10) | collective-permute-done | bytes 131104 | tf_op jit(solution)/shard_map/ppermute | solution.py:224
  77.6 0.8 add_bitcast_fusion
  (6 shorter events, 0.0 us)
Async XLA Ops:
  0.0 29.9 %collective-permute-start.1 = (bf16[48,5120]{1,0:T(8,128)(2,1)}, bf16[48,5120]{1,0:T(8,128)(2,1)S(1)}, u32[]{:S(2)}, u32[]{:S(2)}) collective-permute-start(bf16[48,5120]{1,0:T(8,128)(2,1)} %bitcast.6), channel_id=1, source_target_pairs={{0,4},{4,0},{8,12},{12,8},{1,5},{5,1},{9,13},{13,9},{2,6},{6,2},{1... | collective-permute-start | bytes 1474568 | tf_op jit(solution)/shard_map/ppermute | solution.py:224
  3.0 27.6 %collective-permute-start.3 = (bf16[48,5120]{1,0:T(8,128)(2,1)}, bf16[48,5120]{1,0:T(8,128)(2,1)}, u32[]{:S(2)}, u32[]{:S(2)}) collective-permute-start(bf16[48,5120]{1,0:T(8,128)(2,1)} %bitcast.7), channel_id=1, source_target_pairs={{4,8},{8,4},{5,9},{9,5},{6,10},{10,6},{7,11},{11,7},{20,24},{24,20... | collective-permute-start | bytes 1474568 | tf_op jit(solution)/shard_map/ppermute | solution.py:224
  7.5 24.6 %collective-permute-start.5 = (bf16[48,1728]{1,0:T(8,128)(2,1)}, bf16[48,1728]{1,0:T(8,128)(2,1)S(1)}, u32[]{:S(2)}, u32[]{:S(2)}) collective-permute-start(bf16[48,1728]{1,0:T(8,128)(2,1)} %get-tuple-element.21), channel_id=1, source_target_pairs={{0,4},{4,0},{8,12},{12,8},{1,5},{5,1},{9,13},{13,9},{2,6},{6,2},{1... | collective-permute-start | bytes 497672 | tf_op jit(solution)/shard_map/ppermute | solution.py:224
  11.1 33.2 %collective-permute-start = (bf16[48,1728]{1,0:T(8,128)(2,1)}, bf16[48,1728]{1,0:T(8,128)(2,1)S(1)}, u32[]{:S(2)}, u32[]{:S(2)}) collective-permute-start(bf16[48,1728]{1,0:T(8,128)(2,1)} %get-tuple-element.17), channel_id=1, source_target_pairs={{0,8},{8,0},{4,12},{12,4},{1,9},{9,1},{5,13},{13,5},{2,10},{10,2},... | collective-permute-start | bytes 497672 | tf_op jit(solution)/shard_map/ppermute | solution.py:224
  11.1 48.2 %collective-permute-start.8 = (bf16[48,1728]{1,0:T(8,128)(2,1)}, bf16[48,1728]{1,0:T(8,128)(2,1)S(1)}, u32[]{:S(2)}, u32[]{:S(2)}) collective-permute-start(bf16[48,1728]{1,0:T(8,128)(2,1)} %get-tuple-element.24), channel_id=1, source_target_pairs={{0,12},{12,0},{4,8},{8,4},{1,13},{13,1},{5,9},{9,5},{2,14},{14,2},... | collective-permute-start | bytes 497672 | tf_op jit(solution)/shard_map/ppermute | solution.py:224
  29.9 13.0 %collective-permute-start.2 = (bf16[48,5120]{1,0:T(8,128)(2,1)S(1)}, bf16[48,5120]{1,0:T(8,128)(2,1)S(1)}, u32[]{:S(2)}, u32[]{:S(2)}) collective-permute-start(bf16[48,5120]{1,0:T(8,128)(2,1)S(1)} %collective-permute-done.1.a), channel_id=1, source_target_pairs={{4,8},{8,4},{5,9},{9,5},{6,10},{10,6},{7,11},{11,7},{20,24},{24,20... | collective-permute-start | bytes 1474568 | tf_op jit(solution)/shard_map/ppermute | solution.py:224
  30.6 13.9 %collective-permute-start.4 = (bf16[48,5120]{1,0:T(8,128)(2,1)}, bf16[48,5120]{1,0:T(8,128)(2,1)S(1)}, u32[]{:S(2)}, u32[]{:S(2)}) collective-permute-start(bf16[48,5120]{1,0:T(8,128)(2,1)} %collective-permute-done.3.a), channel_id=1, source_target_pairs={{8,12},{4,0},{9,13},{5,1},{10,14},{6,2},{11,15},{7,3},{24,28},{20,... | collective-permute-start | bytes 1474568 | tf_op jit(solution)/shard_map/ppermute | solution.py:224
  42.9 34.6 %copy-start = (f32[512,128]{1,0:T(8,128)S(1)}, f32[512,128]{1,0:T(8,128)}, u32[]{:S(2)}) copy-start(f32[512,128]{1,0:T(8,128)} %get-tuple-element.16) | copy-start | bytes 786436
  42.9 16.4 %collective-permute-start.9 = (bf16[48,5120]{1,0:T(8,128)(2,1)S(1)}, bf16[48,5120]{1,0:T(8,128)(2,1)S(1)}, u32[]{:S(2)}, u32[]{:S(2)}) collective-permute-start(bf16[48,5120]{1,0:T(8,128)(2,1)S(1)} %collective-permute-done.2.a), channel_id=1, source_target_pairs={{8,12},{4,0},{9,13},{5,1},{10,14},{6,2},{11,15},{7,3},{24,28},{20,... | collective-permute-start | bytes 1474568 | tf_op jit(solution)/shard_map/ppermute | solution.py:224
  55.7 16.3 %collective-permute-start.6 = (bf16[512,128]{1,0:T(8,128)(2,1)}, bf16[512,128]{1,0:T(8,128)(2,1)S(1)}, u32[]{:S(2)}, u32[]{:S(2)}) collective-permute-start(bf16[512,128]{1,0:T(8,128)(2,1)} %get-tuple-element.22), channel_id=1, source_target_pairs={{0,4},{4,0},{8,12},{12,8},{1,5},{5,1},{9,13},{13,9},{2,6},{6,2},{1... | collective-permute-start | bytes 393224 | tf_op jit(solution)/shard_map/ppermute | solution.py:224
  58.2 13.8 %collective-permute-start.7 = (bf16[512,128]{1,0:T(8,128)(2,1)}, bf16[512,128]{1,0:T(8,128)(2,1)S(1)}, u32[]{:S(2)}, u32[]{:S(2)}) collective-permute-start(bf16[512,128]{1,0:T(8,128)(2,1)} %get-tuple-element.23), channel_id=1, source_target_pairs={{0,8},{8,0},{4,12},{12,4},{1,9},{9,1},{5,13},{13,5},{2,10},{10,2},... | collective-permute-start | bytes 393224 | tf_op jit(solution)/shard_map/ppermute | solution.py:224
  70.5 7.1 %collective-permute-start.10 = (bf16[512,128]{1,0:T(8,128)(2,1)}, bf16[512,128]{1,0:T(8,128)(2,1)S(1)}, u32[]{:S(2)}, u32[]{:S(2)}) collective-permute-start(bf16[512,128]{1,0:T(8,128)(2,1)} %shard_map.59), channel_id=1, source_target_pairs={{0,12},{12,0},{4,8},{8,4},{1,13},{13,1},{5,9},{9,5},{2,14},{14,2},... | collective-permute-start | bytes 393224 | tf_op jit(solution)/shard_map/ppermute | solution.py:224

commit v6 on v5

--- a/solution.py
+++ b/solution.py
@@ -102,10 +102,11 @@
 def split_kernel(counts, place, grads, *outs):
     tokens = grads.shape[0]
     rows = outs[0].shape[1]
-    live = lax.broadcasted_iota(jnp.int32, (tokens, rows), 0) < counts[0]
+    live = lax.broadcasted_iota(jnp.int32, (tokens, 1), 0) < counts[0]
+    live = jnp.where(live, 1.0, 0.0).astype(BF16)
     for block in range(len(outs)):
         part = grads[:, block * rows : (block + 1) * rows]
-        part = jnp.where(live, part.astype(F32), 0.0).astype(BF16)
+        part = part * live
         for k, out in enumerate(outs):
 
             @pl.when(place[0] == block ^ k)

time: 78.6 us -> 78.5 us (level)
  no operation moved by 1% of the time
where the time goes in v6:
time: 78.5 us; the launch traced here: 78.3 us
  Pallas kernels  51.8 us (66%)
  starting transfers between devices  19.2 us (24%)
  waiting for transfers between devices  5.82 us (7%)
    ppermute x11, starting transfers between devices, send(): return lax.ppermute(x, 'blk', pairs)  19.2 us
    pallas_call x1, Pallas kernels, line_shards(): pl.pallas_call(functools.partial(first_kernel, tile, chunk), in_specs=[SM...  16.4 us
    pallas_call x1, Pallas kernels, term(): pl.pallas_call(body, in_specs=[SMEM, VMEM, ANY] + [VMEM] * 4, scratch_sha...  11.1 us
    pallas_call x1, Pallas kernels, term(): pl.pallas_call(body, in_specs=[SMEM] + [VMEM] * 6 + [ANY], input_output_a...  11.1 us
    pallas_call x1, Pallas kernels, term(): pl.pallas_call(body, in_specs=[SMEM] + [VMEM] * 5, scratch_shapes=scratch...  10.8 us
    ppermute x11, waiting for transfers between devices, send(): return lax.ppermute(x, 'blk', pairs)  5.82 us
    pallas_call x1, Pallas kernels, line_shards(): pl.pallas_call(split_kernel, in_specs=[SMEM, SMEM, VMEM], out_specs=[VMEM...  2.32 us
  transfers between devices with their start and end apart: 11, of which 2 were waited for; matrix products, arithmetic and copies ran while one was open for 0% of the time, Pallas kernels for 66%

profile of v6, /device:TPU:0, one launch (start us, length us, event | category | flops | bytes accessed | tf_op | source)
XLA Modules:
  0.0 78.3 jit_solution(9333576118628502890)
XLA Ops:
  0.0 3.0 %collective-permute-start.1 = (bf16[48,5120]{1,0:T(8,128)(2,1)}, bf16[48,5120]{1,0:T(8,128)(2,1)S(1)}, u32[]{:S(2)}, u32[]{:S(2)}) collective-permute-start(bf16[48,5120]{1,0:T(8,128)(2,1)} %bitcast.6), channel_id=1, source_target_pairs={{0,4},{4,0},{8,12},{12,8},{1,5},{5,1},{9,13},{13,9},{2,6},{6,2},{1... | collective-permute-start | bytes 1474568 | tf_op jit(solution)/shard_map/ppermute | solution.py:225
  3.0 1.4 %collective-permute-start.3 = (bf16[48,5120]{1,0:T(8,128)(2,1)}, bf16[48,5120]{1,0:T(8,128)(2,1)}, u32[]{:S(2)}, u32[]{:S(2)}) collective-permute-start(bf16[48,5120]{1,0:T(8,128)(2,1)} %bitcast.7), channel_id=1, source_target_pairs={{4,8},{8,4},{5,9},{9,5},{6,10},{10,6},{7,11},{11,7},{20,24},{24,20... | collective-permute-start | bytes 1474568 | tf_op jit(solution)/shard_map/ppermute | solution.py:225
  5.1 2.3 %shard_map.55 = (bf16[48,1728]{1,0:T(8,128)(2,1)}, bf16[48,1728]{1,0:T(8,128)(2,1)}, bf16[48,1728]{1,0:T(8,128)(2,1)}, bf16[48,1728]{1,0:T(8,128)(2,1)}) custom-call(s32[1]{0:T(128)S(6)} %copy.8.counts, s32[1]{0:T(128)} %bitcast.place, bf16[48,6912]{1,0:T(8,128)(2,1)} %bitcast.5), custom_call_target="tpu_custom_call" | custom-call | tf_op jit(solution)/shard_map/pallas_call | solution.py:229
  7.4 3.6 %collective-permute-start.5 = (bf16[48,1728]{1,0:T(8,128)(2,1)}, bf16[48,1728]{1,0:T(8,128)(2,1)S(1)}, u32[]{:S(2)}, u32[]{:S(2)}) collective-permute-start(bf16[48,1728]{1,0:T(8,128)(2,1)} %get-tuple-element.21), channel_id=1, source_target_pairs={{0,4},{4,0},{8,12},{12,8},{1,5},{5,1},{9,13},{13,9},{2,6},{6,2},{1... | collective-permute-start | bytes 497672 | tf_op jit(solution)/shard_map/ppermute | solution.py:225
  11.0 0.0 collective-permute-start
  11.1 2.4 %collective-permute-start.8 = (bf16[48,1728]{1,0:T(8,128)(2,1)}, bf16[48,1728]{1,0:T(8,128)(2,1)S(1)}, u32[]{:S(2)}, u32[]{:S(2)}) collective-permute-start(bf16[48,1728]{1,0:T(8,128)(2,1)} %get-tuple-element.24), channel_id=1, source_target_pairs={{0,12},{12,0},{4,8},{8,4},{1,13},{13,1},{5,9},{9,5},{2,14},{14,2},... | collective-permute-start | bytes 497672 | tf_op jit(solution)/shard_map/ppermute | solution.py:225
  13.4 16.4 %shard_map.56 = (f32[512,128]{1,0:T(8,128)}, f32[1728,5120]{1,0:T(8,128)S(1)}, bf16[5120,128]{1,0:T(8,128)(2,1)S(1)}, bf16[512,1728]{1,0:T(8,128)(2,1)S(1)}) custom-call(s32[2]{0:T(128)} %seeds.1, s32[1]{0:T(128)} %bitcast.place, bf16[48,1728]{1,0:T(8,128)(2,1)} %get-tuple-element.15.grads, bf16[48,5120]{1,0:T(8,128)(2,1)} %bitcast.8, f32[1728,5120]{1,0:T(8,128)} %moment.1), custom_call_target="tpu_custom_call" | custom-call | flops 9059696640 | bytes 35389440 | tf_op jit(solution)/shard_map/pallas_call | solution.py:239
  29.8 0.0 collective-permute-done.1.a
  29.8 0.7 collective-permute-start.2
  30.5 0.0 collective-permute-done.3.a
  30.5 1.5 %collective-permute-start.4 = (bf16[48,5120]{1,0:T(8,128)(2,1)}, bf16[48,5120]{1,0:T(8,128)(2,1)S(1)}, u32[]{:S(2)}, u32[]{:S(2)}) collective-permute-start(bf16[48,5120]{1,0:T(8,128)(2,1)} %collective-permute-done.3.a), channel_id=1, source_target_pairs={{8,12},{4,0},{9,13},{5,1},{10,14},{6,2},{11,15},{7,3},{24,28},{20,... | collective-permute-start | bytes 1474568 | tf_op jit(solution)/shard_map/ppermute | solution.py:225
  32.0 0.0 collective-permute-done.5.g
  32.0 10.8 %shard_map.57.refs_0_ = bf16[512,128]{1,0:T(8,128)(2,1)} custom-call(s32[1]{0:T(128)} %bitcast.place, bf16[48,1728]{1,0:T(8,128)(2,1)S(1)} %collective-permute-done.5.g, bf16[48,5120]{1,0:T(8,128)(2,1)S(1)} %collective-permute-done.1.a, f32[1728,5120]{1,0:T(8,128)S(1)} %get-tuple-element.18.w, bf16[5120,128]{1,0:T(8,128)(2,1)S(1)} %get-tuple-element.19.c, ...), custom_call_target="tpu_custom_call" | custom-call | flops 9059696640 | bytes 35389440 | tf_op jit(solution)/shard_map/pallas_call | solution.py:274
  42.9 1.4 %collective-permute-start.9 = (bf16[48,5120]{1,0:T(8,128)(2,1)S(1)}, bf16[48,5120]{1,0:T(8,128)(2,1)S(1)}, u32[]{:S(2)}, u32[]{:S(2)}) collective-permute-start(bf16[48,5120]{1,0:T(8,128)(2,1)S(1)} %collective-permute-done.2.a), channel_id=1, source_target_pairs={{8,12},{4,0},{9,13},{5,1},{10,14},{6,2},{11,15},{7,3},{24,28},{20,... | collective-permute-start | bytes 1474568 | tf_op jit(solution)/shard_map/ppermute | solution.py:225
  44.3 0.0 collective-permute-done.g
  44.3 0.2 collective-permute-done.4.b
  44.5 11.1 %shard_map.58 = (bf16[512,128]{1,0:T(8,128)(2,1)}, bf16[512,128]{1,0:T(8,128)(2,1)}) custom-call(s32[1]{0:T(128)} %bitcast.place, bf16[48,1728]{1,0:T(8,128)(2,1)S(1)} %collective-permute-done.g, bf16[48,5120]{1,0:T(8,128)(2,1)S(1)} %collective-permute-done.2.a, bf16[48,5120]{1,0:T(8,128)(2,1)S(1)} %collective-permute-done.4.b, ...), custom_call_target="tpu_custom_call", output_to_operand_aliasing={{1}: (7, {})} | custom-call | flops 9059696640 | bytes 35389440 | tf_op jit(solution)/shard_map/pallas_call | solution.py:290
  55.6 2.5 %collective-permute-start.6 = (bf16[512,128]{1,0:T(8,128)(2,1)}, bf16[512,128]{1,0:T(8,128)(2,1)S(1)}, u32[]{:S(2)}, u32[]{:S(2)}) collective-permute-start(bf16[512,128]{1,0:T(8,128)(2,1)} %get-tuple-element.22), channel_id=1, source_target_pairs={{0,4},{4,0},{8,12},{12,8},{1,5},{5,1},{9,13},{13,9},{2,6},{6,2},{1... | collective-permute-start | bytes 393224 | tf_op jit(solution)/shard_map/ppermute | solution.py:225
  58.1 1.2 %collective-permute-start.7 = (bf16[512,128]{1,0:T(8,128)(2,1)}, bf16[512,128]{1,0:T(8,128)(2,1)S(1)}, u32[]{:S(2)}, u32[]{:S(2)}) collective-permute-start(bf16[512,128]{1,0:T(8,128)(2,1)} %get-tuple-element.23), channel_id=1, source_target_pairs={{0,8},{8,0},{4,12},{12,4},{1,9},{9,1},{5,13},{13,5},{2,10},{10,2},... | collective-permute-start | bytes 393224 | tf_op jit(solution)/shard_map/ppermute | solution.py:225
  59.3 0.0 collective-permute-done.8.g
  59.3 11.1 %shard_map.59 = bf16[512,128]{1,0:T(8,128)(2,1)} custom-call(s32[1]{0:T(128)} %bitcast.place, bf16[48,1728]{1,0:T(8,128)(2,1)S(1)} %collective-permute-done.8.g, bf16[48,5120]{1,0:T(8,128)(2,1)} %collective-permute-done.3.a, bf16[48,5120]{1,0:T(8,128)(2,1)S(1)} %collective-permute-done.9.b, f32[1728,5120]{1,0:T(8,128)S(1)} %get-tuple-element.18.w, ...), custom_call_target="tpu_custom_call" | custom-call | flops 9059696640 | bytes 35389440 | tf_op jit(solution)/shard_map/pallas_call | solution.py:285
  70.4 1.5 %collective-permute-start.10 = (bf16[512,128]{1,0:T(8,128)(2,1)}, bf16[512,128]{1,0:T(8,128)(2,1)S(1)}, u32[]{:S(2)}, u32[]{:S(2)}) collective-permute-start(bf16[512,128]{1,0:T(8,128)(2,1)} %shard_map.59), channel_id=1, source_target_pairs={{0,12},{12,0},{4,8},{8,4},{1,13},{13,1},{5,9},{9,5},{2,14},{14,2},... | collective-permute-start | bytes 393224 | tf_op jit(solution)/shard_map/ppermute | solution.py:225
  71.9 5.6 %collective-permute-done.10 = bf16[512,128]{1,0:T(8,128)(2,1)S(1)} collective-permute-done((bf16[512,128]{1,0:T(8,128)(2,1)}, bf16[512,128]{1,0:T(8,128)(2,1)S(1)}, u32[]{:S(2)}, u32[]{:S(2)}) %collective-permute-start.10) | collective-permute-done | bytes 131104 | tf_op jit(solution)/shard_map/ppermute | solution.py:225
  77.5 0.8 add_bitcast_fusion
  (6 shorter events, 0.0 us)
Async XLA Ops:
  0.0 29.8 %collective-permute-start.1 = (bf16[48,5120]{1,0:T(8,128)(2,1)}, bf16[48,5120]{1,0:T(8,128)(2,1)S(1)}, u32[]{:S(2)}, u32[]{:S(2)}) collective-permute-start(bf16[48,5120]{1,0:T(8,128)(2,1)} %bitcast.6), channel_id=1, source_target_pairs={{0,4},{4,0},{8,12},{12,8},{1,5},{5,1},{9,13},{13,9},{2,6},{6,2},{1... | collective-permute-start | bytes 1474568 | tf_op jit(solution)/shard_map/ppermute | solution.py:225
  3.0 27.5 %collective-permute-start.3 = (bf16[48,5120]{1,0:T(8,128)(2,1)}, bf16[48,5120]{1,0:T(8,128)(2,1)}, u32[]{:S(2)}, u32[]{:S(2)}) collective-permute-start(bf16[48,5120]{1,0:T(8,128)(2,1)} %bitcast.7), channel_id=1, source_target_pairs={{4,8},{8,4},{5,9},{9,5},{6,10},{10,6},{7,11},{11,7},{20,24},{24,20... | collective-permute-start | bytes 1474568 | tf_op jit(solution)/shard_map/ppermute | solution.py:225
  7.4 24.6 %collective-permute-start.5 = (bf16[48,1728]{1,0:T(8,128)(2,1)}, bf16[48,1728]{1,0:T(8,128)(2,1)S(1)}, u32[]{:S(2)}, u32[]{:S(2)}) collective-permute-start(bf16[48,1728]{1,0:T(8,128)(2,1)} %get-tuple-element.21), channel_id=1, source_target_pairs={{0,4},{4,0},{8,12},{12,8},{1,5},{5,1},{9,13},{13,9},{2,6},{6,2},{1... | collective-permute-start | bytes 497672 | tf_op jit(solution)/shard_map/ppermute | solution.py:225
  11.0 33.2 %collective-permute-start = (bf16[48,1728]{1,0:T(8,128)(2,1)}, bf16[48,1728]{1,0:T(8,128)(2,1)S(1)}, u32[]{:S(2)}, u32[]{:S(2)}) collective-permute-start(bf16[48,1728]{1,0:T(8,128)(2,1)} %get-tuple-element.17), channel_id=1, source_target_pairs={{0,8},{8,0},{4,12},{12,4},{1,9},{9,1},{5,13},{13,5},{2,10},{10,2},... | collective-permute-start | bytes 497672 | tf_op jit(solution)/shard_map/ppermute | solution.py:225
  11.1 48.2 %collective-permute-start.8 = (bf16[48,1728]{1,0:T(8,128)(2,1)}, bf16[48,1728]{1,0:T(8,128)(2,1)S(1)}, u32[]{:S(2)}, u32[]{:S(2)}) collective-permute-start(bf16[48,1728]{1,0:T(8,128)(2,1)} %get-tuple-element.24), channel_id=1, source_target_pairs={{0,12},{12,0},{4,8},{8,4},{1,13},{13,1},{5,9},{9,5},{2,14},{14,2},... | collective-permute-start | bytes 497672 | tf_op jit(solution)/shard_map/ppermute | solution.py:225
  29.8 13.0 %collective-permute-start.2 = (bf16[48,5120]{1,0:T(8,128)(2,1)S(1)}, bf16[48,5120]{1,0:T(8,128)(2,1)S(1)}, u32[]{:S(2)}, u32[]{:S(2)}) collective-permute-start(bf16[48,5120]{1,0:T(8,128)(2,1)S(1)} %collective-permute-done.1.a), channel_id=1, source_target_pairs={{4,8},{8,4},{5,9},{9,5},{6,10},{10,6},{7,11},{11,7},{20,24},{24,20... | collective-permute-start | bytes 1474568 | tf_op jit(solution)/shard_map/ppermute | solution.py:225
  30.5 13.9 %collective-permute-start.4 = (bf16[48,5120]{1,0:T(8,128)(2,1)}, bf16[48,5120]{1,0:T(8,128)(2,1)S(1)}, u32[]{:S(2)}, u32[]{:S(2)}) collective-permute-start(bf16[48,5120]{1,0:T(8,128)(2,1)} %collective-permute-done.3.a), channel_id=1, source_target_pairs={{8,12},{4,0},{9,13},{5,1},{10,14},{6,2},{11,15},{7,3},{24,28},{20,... | collective-permute-start | bytes 1474568 | tf_op jit(solution)/shard_map/ppermute | solution.py:225
  42.9 34.6 %copy-start = (f32[512,128]{1,0:T(8,128)S(1)}, f32[512,128]{1,0:T(8,128)}, u32[]{:S(2)}) copy-start(f32[512,128]{1,0:T(8,128)} %get-tuple-element.16) | copy-start | bytes 786436
  42.9 16.4 %collective-permute-start.9 = (bf16[48,5120]{1,0:T(8,128)(2,1)S(1)}, bf16[48,5120]{1,0:T(8,128)(2,1)S(1)}, u32[]{:S(2)}, u32[]{:S(2)}) collective-permute-start(bf16[48,5120]{1,0:T(8,128)(2,1)S(1)} %collective-permute-done.2.a), channel_id=1, source_target_pairs={{8,12},{4,0},{9,13},{5,1},{10,14},{6,2},{11,15},{7,3},{24,28},{20,... | collective-permute-start | bytes 1474568 | tf_op jit(solution)/shard_map/ppermute | solution.py:225
  55.6 16.3 %collective-permute-start.6 = (bf16[512,128]{1,0:T(8,128)(2,1)}, bf16[512,128]{1,0:T(8,128)(2,1)S(1)}, u32[]{:S(2)}, u32[]{:S(2)}) collective-permute-start(bf16[512,128]{1,0:T(8,128)(2,1)} %get-tuple-element.22), channel_id=1, source_target_pairs={{0,4},{4,0},{8,12},{12,8},{1,5},{5,1},{9,13},{13,9},{2,6},{6,2},{1... | collective-permute-start | bytes 393224 | tf_op jit(solution)/shard_map/ppermute | solution.py:225
  58.1 13.8 %collective-permute-start.7 = (bf16[512,128]{1,0:T(8,128)(2,1)}, bf16[512,128]{1,0:T(8,128)(2,1)S(1)}, u32[]{:S(2)}, u32[]{:S(2)}) collective-permute-start(bf16[512,128]{1,0:T(8,128)(2,1)} %get-tuple-element.23), channel_id=1, source_target_pairs={{0,8},{8,0},{4,12},{12,4},{1,9},{9,1},{5,13},{13,5},{2,10},{10,2},... | collective-permute-start | bytes 393224 | tf_op jit(solution)/shard_map/ppermute | solution.py:225
  70.4 7.1 %collective-permute-start.10 = (bf16[512,128]{1,0:T(8,128)(2,1)}, bf16[512,128]{1,0:T(8,128)(2,1)S(1)}, u32[]{:S(2)}, u32[]{:S(2)}) collective-permute-start(bf16[512,128]{1,0:T(8,128)(2,1)} %shard_map.59), channel_id=1, source_target_pairs={{0,12},{12,0},{4,8},{8,4},{1,13},{13,1},{5,9},{9,5},{2,14},{14,2},... | collective-permute-start | bytes 393224 | tf_op jit(solution)/shard_map/ppermute | solution.py:225
